TPU v7x, 32 devices: a whole 2x2x4 slice. The times are simulated.
32 devices in a mesh: rep: 8 (over y, x, core), shard: 4 (over z).
Axes of the slice: x: 2, y: 2, z: 4, core: 2. Of those that a mesh axis runs over, the one named last changes fastest.
Arguments:
- prompt_in: bfloat16 [8, 1024, 2048], P('rep', 'shard'), may hold values from -6 to 6
- cont_in: bfloat16 [8, 8, 96, 2048], P('rep', 'shard'), may hold values from -6 to 6
- cotan_prompt: bfloat16 [8, 1024, 2048], P('rep', 'shard'), may hold values from -6 to 6
- cotan_cont: bfloat16 [8, 8, 96, 2048], P('rep', 'shard'), may hold values from -6 to 6
- routes_attn_p: int32 [8, 1024, 2], P('rep', 'shard'), may hold values from 0 to 3, all different within a row; in each aligned block of 256 rows (0 to 255, 256 to 511, ..., all dimensions but the last counted through in order) at most 136 rows name the same one
- routes_attn_c: int32 [8, 8, 96, 2], P('rep', 'shard'), may hold values from 0 to 3, all different within a row; in each aligned block of 192 rows (0 to 191, 192 to 383, ..., all dimensions but the last counted through in order) at most 104 rows name the same one
- routes_ffn_p: int32 [8, 1024, 2], P('rep', 'shard'), may hold values from 0 to 3, all different within a row; in each aligned block of 256 rows (0 to 255, 256 to 511, ..., all dimensions but the last counted through in order) at most 136 rows name the same one
- routes_ffn_c: int32 [8, 8, 96, 2], P('rep', 'shard'), may hold values from 0 to 3, all different within a row; in each aligned block of 192 rows (0 to 191, 192 to 383, ..., all dimensions but the last counted through in order) at most 104 rows name the same one
- adapter_pick: int32 [8], P('rep'), may hold values from 0 to 7
- norm_gains: bfloat16 [2, 2048], replicated, may hold values from 0.5 to 1.5
- router_attn: bfloat16 [2048, 4], replicated, may hold values from -0.09375 to 0.09375
- router_ffn: bfloat16 [2048, 4], replicated, may hold values from -0.09375 to 0.09375
- w_kv: bfloat16 [2, 2048, 2048], P(None, None, 'shard'), may hold values from -0.125 to 0.125
- w_query: bfloat16 [4, 2048, 2048], P(None, None, 'shard'), may hold values from -0.125 to 0.125
- w_out: bfloat16 [4, 2048, 2048], P(None, None, 'shard'), may hold values from -0.5 to 0.5
- w_gate_up: bfloat16 [4, 2, 2048, 5632], P(None, None, None, 'shard'), may hold values from -0.125 to 0.125
- w_down: bfloat16 [4, 5632, 2048], P(None, 'shard'), may hold values from -0.078125 to 0.078125
- ada_in: bfloat16 [8, 6, 16, 2048], P(None, None, None, 'shard'), may hold values from -0.125 to 0.125
- ada_out: bfloat16 [8, 5, 16, 2048], P(None, None, None, 'shard'), may hold values from -0.75 to 0.75
- ada_down: bfloat16 [8, 16, 5632], P(None, None, 'shard'), may hold values from -0.078125 to 0.078125
- ada_ffn: bfloat16 [8, 2, 16, 5632], P(None, None, None, 'shard'), may hold values from -0.75 to 0.75
Outputs:
- out_prompt: bfloat16 [8, 1024, 2048], P('rep', 'shard')
- out_cont: bfloat16 [8, 8, 96, 2048], P('rep', 'shard')
- grad_prompt: float32 [8, 1024, 2048], P('rep', 'shard')
- grad_cont: float32 [8, 8, 96, 2048], P('rep', 'shard')
- grad_ada_in: float32 [8, 6, 16, 2048], P(None, None, None, 'shard')
- grad_ada_out: float32 [8, 5, 16, 2048], P(None, None, None, 'shard')
- grad_ada_down: float32 [8, 16, 5632], P(None, None, 'shard')
- grad_ada_ffn: float32 [8, 2, 16, 5632], P(None, None, None, 'shard')
Inputs may be any that keep to these rules, and one draw needn't show every extreme that they name: `routes_attn_p`: in each aligned block of 256 prompt rows, no attention expert is named by more than 136 rows, a bound that some block reaches; a row names 2 different experts. `routes_attn_c`: in each aligned block of 192 continuation rows, no attention expert is named by more than 104 rows, a bound that some block reaches; a row names 2 different experts. `routes_ffn_p`: in each aligned block of 256 prompt rows, no feed-forward expert is named by more than 136 rows, a bound that some block reaches; a row names 2 different experts. `routes_ffn_c`: in each aligned block of 192 continuation rows, no feed-forward expert is named by more than 104 rows, a bound that some block reaches; a row names 2 different experts.
All inputs are finite; a program needn't handle non-finite values.
Results may differ from a plain program's by a relative error of at most 0.019.
Values may be sent and summed in bfloat16 or wider, within the bound.
No kernel may reach another device: no remote copies, remote signals or barrier semaphores. Data moves between devices by JAX's collectives and lax.ppermute only.
A program may use at most 960 MiB of HBM per device.

v0:
```python
import jax
import jax.numpy as jnp
from jax import lax
from jax.sharding import PartitionSpec as P

HEADS = 16
HD = 128


EPSILON = 1e-05
HIGHEST = lax.Precision.HIGHEST
NEG_FILL = -1e30


def norm_rows(values, scaling):
    inverse = lax.rsqrt(jnp.mean(values * values, axis=-1, keepdims=True) + EPSILON)
    return (values * inverse * scaling, inverse)


def norm_back(values, inverse, scaling, upstream):
    weighted = upstream * scaling
    inner_mean = jnp.mean(weighted * values, axis=-1, keepdims=True)
    return inverse * weighted - values * (inverse * inverse * inverse) * inner_mean


def exact_mm(former, latter):
    return jnp.dot(former, latter, precision=HIGHEST)


def capacity(block_rows, experts, top_count):
    return min(block_rows, ((block_rows * top_count + experts - 1) // experts + 7) // 8 * 8 + 8)


def slot_table(routes, experts, slot_cap, offset):
    row_count = routes.shape[0]
    labels = jnp.arange(experts, dtype=jnp.int32)
    hit_table = (routes[:, :, None] == labels[None, None, :]).astype(jnp.int32)
    member = jnp.sum(hit_table, axis=1)
    picked = jnp.sum(
        hit_table * jnp.arange(routes.shape[1], dtype=jnp.int32)[None, :, None], axis=1
    )
    ranked = jnp.cumsum(member, axis=0) - 1
    places = jnp.arange(slot_cap, dtype=jnp.int32)
    matched = ((member[:, :, None] == 1) & (ranked[:, :, None] == places[None, None, :])).astype(
        jnp.int32
    )
    row_ids = jnp.arange(row_count, dtype=jnp.int32)
    source = jnp.sum(matched * row_ids[:, None, None], axis=0) + offset
    which_top = jnp.sum(matched * picked[:, :, None], axis=0)
    filled = jnp.sum(matched, axis=0)
    return (source, which_top, filled)


def route_tables(routes_one, routes_two, experts, offset):
    top_count = routes_one.shape[1]
    table_one = slot_table(
        routes_one, experts, capacity(routes_one.shape[0], experts, top_count), 0
    )
    table_two = slot_table(
        routes_two, experts, capacity(routes_two.shape[0], experts, top_count), offset
    )
    return tuple(
        (jnp.concatenate([former, latter], axis=1) for former, latter in zip(table_one, table_two))
    )


def route_shares(logits, routes):
    return jax.nn.softmax(jnp.take_along_axis(logits, routes, axis=1), axis=-1)


def shares_back(shares, routes, experts, d_shares):
    d_chosen = shares * (d_shares - jnp.sum(shares * d_shares, axis=-1, keepdims=True))
    onehot = (routes[:, :, None] == jnp.arange(experts, dtype=jnp.int32)[None, None, :]).astype(
        jnp.float32
    )
    return jnp.sum(d_chosen[:, :, None] * onehot, axis=1)


def visible(q_seq, q_flat, key_seq, key_flat):
    same_seq = (key_seq[None, :] == 0) | (key_seq[None, :] == q_seq[:, None])
    return same_seq & (key_flat[None, :] <= q_flat[:, None])


def attend_forward(queries, q_seq, q_flat, all_kv, key_seq, key_flat):
    slot_count = queries.shape[0]
    head_q = queries.reshape(slot_count, HEADS, HD)
    head_k = all_kv[:, 0].reshape(-1, HEADS, HD)
    head_v = all_kv[:, 1].reshape(-1, HEADS, HD)
    allowed = visible(q_seq, q_flat, key_seq, key_flat)
    scores = jnp.einsum(
        "shd,khd->hsk", head_q, head_k, preferred_element_type=jnp.float32
    ) * HD ** (-0.5)
    scores = jnp.where(allowed[None], scores, NEG_FILL)
    row_max = jnp.max(scores, axis=-1, keepdims=True)
    exp_rows = jnp.exp(scores - row_max)
    row_sum = jnp.sum(exp_rows, axis=-1, keepdims=True)
    prob_rows = (exp_rows / row_sum).astype(jnp.bfloat16)
    mixture = jnp.einsum("hsk,khd->shd", prob_rows, head_v, preferred_element_type=jnp.float32)
    return (
        mixture.reshape(slot_count, HEADS * HD).astype(jnp.bfloat16),
        (row_max + jnp.log(row_sum))[:, :, 0],
    )


def attend_backward(queries, grad_out, log_total, q_seq, q_flat, all_kv, key_seq, key_flat):
    slot_count = queries.shape[0]
    scale_qk = HD ** (-0.5)
    head_q = queries.reshape(slot_count, HEADS, HD)
    head_g = grad_out.reshape(slot_count, HEADS, HD)
    head_k = all_kv[:, 0].reshape(-1, HEADS, HD)
    head_v = all_kv[:, 1].reshape(-1, HEADS, HD)
    allowed = visible(q_seq, q_flat, key_seq, key_flat)
    scores = (
        jnp.einsum("shd,khd->hsk", head_q, head_k, preferred_element_type=jnp.float32) * scale_qk
    )
    prob_rows = jnp.where(allowed[None], jnp.exp(scores - log_total[:, :, None]), 0.0)
    d_prob = jnp.einsum("shd,khd->hsk", head_g, head_v, preferred_element_type=jnp.float32)
    d_scores = (prob_rows * (d_prob - jnp.sum(prob_rows * d_prob, axis=-1, keepdims=True))).astype(
        jnp.bfloat16
    )
    d_query = (
        jnp.einsum("hsk,khd->shd", d_scores, head_k, preferred_element_type=jnp.float32) * scale_qk
    )
    d_keys = (
        jnp.einsum("hsk,shd->khd", d_scores, head_q, preferred_element_type=jnp.float32) * scale_qk
    )
    d_values = jnp.einsum(
        "hsk,shd->khd", prob_rows.astype(jnp.bfloat16), head_g, preferred_element_type=jnp.float32
    )
    key_count = head_k.shape[0]
    return (
        d_query.reshape(slot_count, HEADS * HD),
        d_keys.reshape(key_count, HEADS * HD),
        d_values.reshape(key_count, HEADS * HD),
    )


def on_device(
    prompt_in,
    cont_in,
    cotan_prompt,
    cotan_cont,
    routes_attn_p,
    routes_attn_c,
    routes_ffn_p,
    routes_ffn_c,
    adapter_pick,
    norm_gains,
    router_attn,
    router_ffn,
    w_kv,
    w_query,
    w_out,
    w_gate_up,
    w_down,
    ada_in,
    ada_out,
    ada_down,
    ada_ffn,
):
    prompt_rows = prompt_in.shape[1]
    cont_count = cont_in.shape[1]
    cont_len = cont_in.shape[2]
    feature_count = prompt_in.shape[2]
    n_attn = w_query.shape[0]
    n_ffn = w_down.shape[0]
    top_count = routes_attn_p.shape[2]
    shard_count = lax.axis_size("shard")
    shard_id = lax.axis_index("shard")
    prompt_total = prompt_rows * shard_count
    cont_rows = cont_count * cont_len
    row_count = prompt_rows + cont_rows
    tokens = jnp.concatenate(
        [prompt_in[0], cont_in[0].reshape(cont_rows, feature_count)], axis=0
    ).astype(jnp.float32)
    upstream = jnp.concatenate(
        [cotan_prompt[0], cotan_cont[0].reshape(cont_rows, feature_count)], axis=0
    ).astype(jnp.float32)
    routes_a = jnp.concatenate(
        [routes_attn_p[0], routes_attn_c[0].reshape(cont_rows, top_count)], axis=0
    )
    routes_f = jnp.concatenate(
        [routes_ffn_p[0], routes_ffn_c[0].reshape(cont_rows, top_count)], axis=0
    )
    chosen_id = adapter_pick[0]
    own_in = lax.dynamic_index_in_dim(ada_in, chosen_id, 0, keepdims=False)
    own_out = lax.dynamic_index_in_dim(ada_out, chosen_id, 0, keepdims=False)
    own_down = lax.dynamic_index_in_dim(ada_down, chosen_id, 0, keepdims=False)
    own_ffn = lax.dynamic_index_in_dim(ada_ffn, chosen_id, 0, keepdims=False)
    gain_one = norm_gains[0].astype(jnp.float32)
    gain_two = norm_gains[1].astype(jnp.float32)
    cont_seq = jnp.repeat(jnp.arange(1, cont_count + 1, dtype=jnp.int32), cont_len)
    cont_flat = prompt_total + shard_id * cont_rows + jnp.arange(cont_rows, dtype=jnp.int32)
    row_seq = jnp.concatenate([jnp.zeros((prompt_rows,), jnp.int32), cont_seq])
    row_flat = jnp.concatenate(
        [shard_id * prompt_rows + jnp.arange(prompt_rows, dtype=jnp.int32), cont_flat]
    )
    key_seq = jnp.concatenate([jnp.zeros((prompt_total,), jnp.int32), cont_seq])
    key_flat = jnp.concatenate([jnp.arange(prompt_total, dtype=jnp.int32), cont_flat])
    full_kv, full_q, full_out, full_in, full_outb, full_down, full_ffn = (
        lax.all_gather(w_kv, "shard", axis=2, tiled=True),
        lax.all_gather(w_query, "shard", axis=2, tiled=True),
        lax.all_gather(w_out, "shard", axis=2, tiled=True),
        lax.all_gather(own_in, "shard", axis=2, tiled=True),
        lax.all_gather(own_out, "shard", axis=2, tiled=True),
        lax.all_gather(own_down, "shard", axis=1, tiled=True),
        lax.all_gather(own_ffn, "shard", axis=2, tiled=True),
    )
    b_out = full_outb.astype(jnp.float32)
    a_in32 = full_in.astype(jnp.float32)
    normed_one, inverse_one = norm_rows(tokens, gain_one)
    input_one = normed_one.astype(jnp.bfloat16)
    low_one = jnp.einsum("nd,jrd->njr", input_one, full_in[:3], preferred_element_type=jnp.float32)
    kv_rows = jnp.einsum(
        "nd,jdk->njk", input_one, full_kv, preferred_element_type=jnp.float32
    ) + jnp.einsum("njr,jrk->njk", low_one[:, 1:3], b_out[1:3], precision=HIGHEST)
    kv_send = kv_rows.astype(jnp.bfloat16)
    prompt_kv = lax.all_gather(kv_send[:prompt_rows], "shard", axis=0, tiled=True)
    all_kv = jnp.concatenate([prompt_kv, kv_send[prompt_rows:]], axis=0)
    shares_attn = route_shares(
        jnp.dot(input_one, router_attn, preferred_element_type=jnp.float32), routes_a
    )
    source_a, which_a, filled_a = route_tables(
        routes_attn_p[0], routes_attn_c[0].reshape(cont_rows, top_count), n_attn, prompt_rows
    )
    gate_a = shares_attn[source_a, which_a] * filled_a.astype(jnp.float32)
    slot_in_a = input_one[source_a]
    low_q = low_one[:, 0][source_a]
    queries = (
        jnp.einsum("esd,edk->esk", slot_in_a, full_q, preferred_element_type=jnp.float32)
        + jnp.einsum("esr,rk->esk", low_q, b_out[0], precision=HIGHEST)
    ).astype(jnp.bfloat16)
    q_seq_all = row_seq[source_a]
    q_flat_all = row_flat[source_a]

    def forward_expert(member):
        return attend_forward(member[0], member[1], member[2], all_kv, key_seq, key_flat)

    attended, log_totals = lax.map(forward_expert, (queries, q_seq_all, q_flat_all))
    low_o = jnp.einsum("esk,rk->esr", attended, full_in[3], preferred_element_type=jnp.float32)
    branch_a = jnp.einsum(
        "esk,ekd->esd", attended, full_out, preferred_element_type=jnp.float32
    ) + jnp.einsum("esr,rd->esd", low_o, b_out[3], precision=HIGHEST)
    attn_rows = (
        jnp.zeros((row_count, feature_count), jnp.float32)
        .at[source_a.reshape(-1)]
        .add((gate_a[:, :, None] * branch_a).reshape(-1, feature_count))
    )
    hidden_one = tokens + attn_rows
    normed_two, inverse_two = norm_rows(hidden_one, gain_two)
    input_two = normed_two.astype(jnp.bfloat16)
    shares_ffn = route_shares(
        jnp.dot(input_two, router_ffn, preferred_element_type=jnp.float32), routes_f
    )
    table_f = route_tables(
        routes_ffn_p[0], routes_ffn_c[0].reshape(cont_rows, top_count), n_ffn, prompt_rows
    )
    source_f, which_f, filled_f = (table_f[0].T, table_f[1].T, table_f[2].T.astype(jnp.float32))
    gate_f = shares_ffn[source_f, which_f] * filled_f
    slot_in_f = input_two[source_f]
    low_rows_ff = jnp.einsum(
        "nd,jrd->njr", input_two, full_in[4:6], preferred_element_type=jnp.float32
    )
    low_ff = low_rows_ff[source_f]

    def fetch_expert(expert):
        return (
            lax.all_gather(w_gate_up[expert], "shard", axis=2, tiled=True),
            lax.all_gather(w_down[expert], "shard", axis=0, tiled=True),
        )

    ffn_b32 = full_ffn.astype(jnp.float32)
    kept_gu = []
    outputs = []
    for expert in range(n_ffn):
        w_gu_full, w_down_full = fetch_expert(expert)
        gate_up = jnp.einsum(
            "sd,jdf->sjf", slot_in_f[:, expert], w_gu_full, preferred_element_type=jnp.float32
        ) + jnp.einsum("sjr,jrf->sjf", low_ff[:, expert], ffn_b32, precision=HIGHEST)
        activated = (jax.nn.silu(gate_up[:, 0]) * gate_up[:, 1]).astype(jnp.bfloat16)
        outputs.append(
            jnp.dot(activated, w_down_full, preferred_element_type=jnp.float32)
            + exact_mm(
                jnp.dot(activated, full_down.T, preferred_element_type=jnp.float32), b_out[4]
            )
        )
        kept_gu.append(gate_up)
    expert_out = jnp.stack(outputs, axis=1)
    ffn_rows = (
        jnp.zeros((row_count, feature_count), jnp.float32)
        .at[source_f.reshape(-1)]
        .add((gate_f[:, :, None] * expert_out).reshape(-1, feature_count))
    )
    layer_out = (hidden_one + ffn_rows).astype(jnp.bfloat16)
    up_slots = upstream[source_f]
    d_gate_f = jnp.sum(up_slots * expert_out, axis=-1) * filled_f
    d_expert = (gate_f[:, :, None] * up_slots).astype(jnp.bfloat16)
    down_a32 = full_down.astype(jnp.float32)
    grad_a_ff = jnp.zeros(full_in[4:6].shape, jnp.float32)
    grad_b_ff = jnp.zeros(full_ffn.shape, jnp.float32)
    grad_a_down = jnp.zeros(full_down.shape, jnp.float32)
    grad_b_down = jnp.zeros(full_outb[4].shape, jnp.float32)
    d_slots = []
    for expert in range(n_ffn):
        w_gu_full, w_down_full = fetch_expert(expert)
        gate_up = kept_gu[expert]
        d_one = d_expert[:, expert]
        sigmoid_g = jax.nn.sigmoid(gate_up[:, 0])
        activated = (gate_up[:, 0] * sigmoid_g * gate_up[:, 1]).astype(jnp.bfloat16)
        low_down = jnp.dot(activated, full_down.T, preferred_element_type=jnp.float32)
        d_low_down = jnp.dot(d_one, full_outb[4].T, preferred_element_type=jnp.float32)
        d_act = jnp.dot(d_one, w_down_full.T, preferred_element_type=jnp.float32) + exact_mm(
            d_low_down, down_a32
        )
        grad_b_down = grad_b_down + exact_mm(low_down.T, d_one.astype(jnp.float32))
        grad_a_down = grad_a_down + exact_mm(d_low_down.T, activated.astype(jnp.float32))
        d_gate_up = jnp.stack(
            [
                d_act * gate_up[:, 1] * sigmoid_g * (1.0 + gate_up[:, 0] * (1.0 - sigmoid_g)),
                d_act * gate_up[:, 0] * sigmoid_g,
            ],
            axis=1,
        ).astype(jnp.bfloat16)
        d_low_ff = jnp.einsum(
            "sjf,jrf->sjr", d_gate_up, full_ffn, preferred_element_type=jnp.float32
        )
        d_slots.append(
            jnp.einsum("sjf,jdf->sd", d_gate_up, w_gu_full, preferred_element_type=jnp.float32)
            + jnp.einsum("sjr,jrd->sd", d_low_ff, a_in32[4:6], precision=HIGHEST)
        )
        grad_b_ff = grad_b_ff + jnp.einsum(
            "sjr,sjf->jrf", low_ff[:, expert], d_gate_up.astype(jnp.float32), precision=HIGHEST
        )
        grad_a_ff = grad_a_ff + jnp.einsum(
            "sjr,sd->jrd", d_low_ff, slot_in_f[:, expert].astype(jnp.float32), precision=HIGHEST
        )
    d_slot_in = jnp.stack(d_slots, axis=1)
    d_shares_f = (
        jnp.zeros(shares_ffn.shape, jnp.float32)
        .at[source_f.reshape(-1), which_f.reshape(-1)]
        .add(d_gate_f.reshape(-1))
    )
    d_logits_f = shares_back(shares_ffn, routes_f, n_ffn, d_shares_f)
    d_input_two = (
        jnp.zeros((row_count, feature_count), jnp.float32)
        .at[source_f.reshape(-1)]
        .add(d_slot_in.reshape(-1, feature_count))
    )
    d_input_two = d_input_two + exact_mm(d_logits_f, router_ffn.astype(jnp.float32).T)
    d_hidden = upstream + norm_back(hidden_one, inverse_two, gain_two, d_input_two)
    d_slots_a = d_hidden[source_a]
    d_gate_a = jnp.sum(d_slots_a * branch_a, axis=-1) * filled_a.astype(jnp.float32)
    d_branch = (gate_a[:, :, None] * d_slots_a).astype(jnp.bfloat16)
    d_low_o = jnp.einsum("esd,rd->esr", d_branch, full_outb[3], preferred_element_type=jnp.float32)
    d_attended = (
        jnp.einsum("esd,ekd->esk", d_branch, full_out, preferred_element_type=jnp.float32)
        + jnp.einsum("esr,rk->esk", d_low_o, a_in32[3], precision=HIGHEST)
    ).astype(jnp.bfloat16)
    grad_b_o = jnp.einsum("esr,esd->rd", low_o, d_branch.astype(jnp.float32), precision=HIGHEST)
    grad_a_o = jnp.einsum("esr,esk->rk", d_low_o, attended.astype(jnp.float32), precision=HIGHEST)

    def backward_expert(carried, member):
        d_query, d_keys, d_values = attend_backward(
            member[0], member[1], member[2], member[3], member[4], all_kv, key_seq, key_flat
        )
        return (carried + jnp.stack([d_keys, d_values], axis=1), d_query)

    kv_start = jnp.zeros((all_kv.shape[0], 2, all_kv.shape[2]), jnp.float32)
    d_kv_all, d_queries = lax.scan(
        backward_expert, kv_start, (queries, d_attended, log_totals, q_seq_all, q_flat_all)
    )
    d_q_b = d_queries.astype(jnp.bfloat16)
    d_low_q = jnp.einsum("esk,rk->esr", d_q_b, full_outb[0], preferred_element_type=jnp.float32)
    d_slot_a = jnp.einsum(
        "esk,edk->esd", d_q_b, full_q, preferred_element_type=jnp.float32
    ) + jnp.einsum("esr,rd->esd", d_low_q, a_in32[0], precision=HIGHEST)
    grad_b_q = jnp.einsum("esr,esk->rk", low_q, d_q_b.astype(jnp.float32), precision=HIGHEST)
    grad_a_q = jnp.einsum("esr,esd->rd", d_low_q, slot_in_a.astype(jnp.float32), precision=HIGHEST)
    prompt_grads = lax.psum_scatter(
        d_kv_all[:prompt_total].astype(jnp.bfloat16), "shard", scatter_dimension=0, tiled=True
    ).astype(jnp.float32)
    d_kv_rows = jnp.concatenate([prompt_grads, d_kv_all[prompt_total:]], axis=0).astype(
        jnp.bfloat16
    )
    d_low_kv = jnp.einsum(
        "njk,jrk->njr", d_kv_rows, full_outb[1:3], preferred_element_type=jnp.float32
    )
    d_input_one = jnp.einsum(
        "njk,jdk->nd", d_kv_rows, full_kv, preferred_element_type=jnp.float32
    ) + jnp.einsum("njr,jrd->nd", d_low_kv, a_in32[1:3], precision=HIGHEST)
    grad_b_kv = jnp.einsum(
        "njr,njk->jrk", low_one[:, 1:3], d_kv_rows.astype(jnp.float32), precision=HIGHEST
    )
    grad_a_kv = jnp.einsum(
        "njr,nd->jrd", d_low_kv, input_one.astype(jnp.float32), precision=HIGHEST
    )
    d_input_one = d_input_one + jnp.zeros((row_count, feature_count), jnp.float32).at[
        source_a.reshape(-1)
    ].add(d_slot_a.reshape(-1, feature_count))
    d_shares_a = (
        jnp.zeros(shares_attn.shape, jnp.float32)
        .at[source_a.reshape(-1), which_a.reshape(-1)]
        .add(d_gate_a.reshape(-1))
    )
    d_logits_a = shares_back(shares_attn, routes_a, n_attn, d_shares_a)
    d_input_one = d_input_one + exact_mm(d_logits_a, router_attn.astype(jnp.float32).T)
    d_tokens = d_hidden + norm_back(tokens, inverse_one, gain_one, d_input_one)
    grad_in = jnp.concatenate([grad_a_q[None], grad_a_kv, grad_a_o[None], grad_a_ff], axis=0)
    grad_out = jnp.concatenate(
        [grad_b_q[None], grad_b_kv, grad_b_o[None], grad_b_down[None]], axis=0
    )
    grad_in, grad_out, grad_down, grad_ffn = (
        lax.psum_scatter(
            grad_in.astype(jnp.bfloat16), "shard", scatter_dimension=2, tiled=True
        ).astype(jnp.float32),
        lax.psum_scatter(
            grad_out.astype(jnp.bfloat16), "shard", scatter_dimension=2, tiled=True
        ).astype(jnp.float32),
        lax.psum_scatter(
            grad_a_down.astype(jnp.bfloat16), "shard", scatter_dimension=1, tiled=True
        ).astype(jnp.float32),
        lax.psum_scatter(
            grad_b_ff.astype(jnp.bfloat16), "shard", scatter_dimension=2, tiled=True
        ).astype(jnp.float32),
    )
    slot_hot = (jnp.arange(ada_in.shape[0], dtype=jnp.int32) == chosen_id).astype(jnp.float32)
    summed = (
        lax.psum(
            (slot_hot[:, None, None, None] * grad_in[None]).astype(jnp.bfloat16), "rep"
        ).astype(jnp.float32),
        lax.psum(
            (slot_hot[:, None, None, None] * grad_out[None]).astype(jnp.bfloat16), "rep"
        ).astype(jnp.float32),
        lax.psum((slot_hot[:, None, None] * grad_down[None]).astype(jnp.bfloat16), "rep").astype(
            jnp.float32
        ),
        lax.psum(
            (slot_hot[:, None, None, None] * grad_ffn[None]).astype(jnp.bfloat16), "rep"
        ).astype(jnp.float32),
    )
    out_prompt = layer_out[:prompt_rows][None]
    out_cont = layer_out[prompt_rows:].reshape(1, cont_count, cont_len, feature_count)
    grad_prompt = d_tokens[:prompt_rows][None]
    grad_cont = d_tokens[prompt_rows:].reshape(1, cont_count, cont_len, feature_count)
    return (
        out_prompt,
        out_cont,
        grad_prompt,
        grad_cont,
        summed[0],
        summed[1],
        summed[2],
        summed[3],
    )


def solution(mesh):
    in_specs = (
        P("rep", "shard", None),
        P("rep", "shard", None, None),
        P("rep", "shard", None),
        P("rep", "shard", None, None),
        P("rep", "shard", None),
        P("rep", "shard", None, None),
        P("rep", "shard", None),
        P("rep", "shard", None, None),
        P("rep"),
        P(),
        P(),
        P(),
        P(None, None, "shard"),
        P(None, None, "shard"),
        P(None, None, "shard"),
        P(None, None, None, "shard"),
        P(None, "shard", None),
        P(None, None, None, "shard"),
        P(None, None, None, "shard"),
        P(None, None, "shard"),
        P(None, None, None, "shard"),
    )
    out_specs = (
        P("rep", "shard", None),
        P("rep", "shard", None, None),
        P("rep", "shard", None),
        P("rep", "shard", None, None),
        P(None, None, None, "shard"),
        P(None, None, None, "shard"),
        P(None, None, "shard"),
        P(None, None, None, "shard"),
    )
    return jax.shard_map(
        on_device, mesh=mesh, in_specs=in_specs, out_specs=out_specs, check_vma=False
    )
```

profile of v0, /device:TPU:0, one launch (start us, length us, event | category | flops | bytes accessed | tf_op | source)
XLA Modules:
  0.0 7667.8 jit_solution(10111958089070224936)
XLA Ops:
  11.5 16.7 all-gather.1
  28.2 30.6 all-gather
  67.6 237.8 %all-gather.27.cloned.1.call-done = bf16[2,2048,2048]{2,1,0:T(8,128)(2,1)} async-done(((bf16[2,2048,512]{2,1,0:T(8,128)(2,1)}), bf16[2,2048,2048]{2,1,0:T(8,128)(2,1)}) %all-gather.27.cloned.1.call-update) | async-done | bytes 16777232 | tf_op jit(solution)/shard_map/all_gather | solution.py:201
  305.4 14.9 fusion.62
  324.9 30.7 fusion.244
  355.7 18.1 fusion.245
  434.1 22.1 all-gather.3
  457.0 19.2 all-gather.5
  514.4 527.5 %all-gather.25.cloned.1.call-done = bf16[4,2048,2048]{2,1,0:T(8,128)(2,1)} async-done(((bf16[4,2048,512]{2,1,0:T(8,128)(2,1)}), bf16[4,2048,2048]{2,1,0:T(8,128)(2,1)}) %all-gather.25.cloned.1.call-update) | async-done | bytes 33554448 | tf_op jit(solution)/shard_map/all_gather | solution.py:202
  1041.9 23.9 fusion.258
  1073.2 198.6 %while.25 = (s32[]{:T(128)}, bf16[4,240,2048]{2,1,0:T(8,128)(2,1)}, f32[4,16,240]{2,1,0:T(8,128)}, s32[1216]{0:T(1024)S(1)}, s32[4,240]{1,0:T(4,128)S(1)}, /*ind...) while((s32[]{:T(128)}, bf16[4,240,2048]{2,1,0:T(8,128)(2,1)}, ...), condition=%wide.region_20.22_spmd, body=%wide.region_17.21_spmd.sunk | while | flops 2429765120 | bytes 122300808 | solution.py:239
  1275.0 327.9 %all-gather.31.cloned.1.call-done = bf16[4,2048,2048]{2,1,0:T(8,128)(2,1)} async-done(((bf16[4,2048,512]{2,1,0:T(8,128)(2,1)}), bf16[4,2048,2048]{2,1,0:T(8,128)(2,1)}) %all-gather.31.cloned.1.call-update) | async-done | bytes 33554448 | tf_op jit(solution)/shard_map/all_gather | solution.py:203
  1603.0 25.0 fusion.259
  1639.1 18.7 scatter_fusion
  1698.2 672.1 %all-gather.33.cloned.1.call-done = bf16[1,2,2048,5632]{3,2,1,0:T(8,128)(2,1)} async-done(((bf16[1,2,2048,1408]{3,2,1,0:T(8,128)(2,1)}), bf16[1,2,2048,5632]{3,2,1,0:T(8,128)(2,1)}) %all-gather.33.cloned.1.call-update) | async-done | bytes 46137360 | tf_op jit(solution)/shard_map/all_gather | solution.py:268
  2370.4 25.9 fusion.41
  2408.5 352.6 %all-gather.35.cloned.1.call-done = bf16[1,5632,2048]{2,1,0:T(8,128)(2,1)} async-done(((bf16[1,1408,2048]{2,1,0:T(8,128)(2,1)}), bf16[1,5632,2048]{2,1,0:T(8,128)(2,1)}) %all-gather.35.cloned.1.call-update) | async-done | bytes 23068688 | tf_op jit(solution)/shard_map/all_gather | solution.py:269
  2776.2 752.6 %all-gather.37.cloned.1.call-done = bf16[1,2,2048,5632]{3,2,1,0:T(8,128)(2,1)} async-done(((bf16[1,2,2048,1408]{3,2,1,0:T(8,128)(2,1)}), bf16[1,2,2048,5632]{3,2,1,0:T(8,128)(2,1)}) %all-gather.37.cloned.1.call-update) | async-done | bytes 46137360 | tf_op jit(solution)/shard_map/all_gather | solution.py:268
  3528.8 26.7 fusion.37
  3567.6 352.0 %all-gather.39.cloned.1.call-done = bf16[1,5632,2048]{2,1,0:T(8,128)(2,1)} async-done(((bf16[1,1408,2048]{2,1,0:T(8,128)(2,1)}), bf16[1,5632,2048]{2,1,0:T(8,128)(2,1)}) %all-gather.39.cloned.1.call-update) | async-done | bytes 23068688 | tf_op jit(solution)/shard_map/all_gather | solution.py:269
  3934.7 752.7 %all-gather.41.cloned.1.call-done = bf16[1,2,2048,5632]{3,2,1,0:T(8,128)(2,1)} async-done(((bf16[1,2,2048,1408]{3,2,1,0:T(8,128)(2,1)}), bf16[1,2,2048,5632]{3,2,1,0:T(8,128)(2,1)}) %all-gather.41.cloned.1.call-update) | async-done | bytes 46137360 | tf_op jit(solution)/shard_map/all_gather | solution.py:268
  4687.4 26.8 fusion.33
  4726.3 351.8 %all-gather.43.cloned.1.call-done = bf16[1,5632,2048]{2,1,0:T(8,128)(2,1)} async-done(((bf16[1,1408,2048]{2,1,0:T(8,128)(2,1)}), bf16[1,5632,2048]{2,1,0:T(8,128)(2,1)}) %all-gather.43.cloned.1.call-update) | async-done | bytes 23068688 | tf_op jit(solution)/shard_map/all_gather | solution.py:269
  5092.9 752.9 %all-gather.45.cloned.1.call-done = bf16[1,2,2048,5632]{3,2,1,0:T(8,128)(2,1)} async-done(((bf16[1,2,2048,1408]{3,2,1,0:T(8,128)(2,1)}), bf16[1,2,2048,5632]{3,2,1,0:T(8,128)(2,1)}) %all-gather.45.cloned.1.call-update) | async-done | bytes 46137360 | tf_op jit(solution)/shard_map/all_gather | solution.py:268
  5845.8 27.4 fusion.29
  5885.3 351.3 %all-gather.47.cloned.1.call-done = bf16[1,5632,2048]{2,1,0:T(8,128)(2,1)} async-done(((bf16[1,1408,2048]{2,1,0:T(8,128)(2,1)}), bf16[1,5632,2048]{2,1,0:T(8,128)(2,1)}) %all-gather.47.cloned.1.call-update) | async-done | bytes 23068688 | tf_op jit(solution)/shard_map/all_gather | solution.py:269
  6261.3 49.2 scatter_fusion.1
  6335.1 13.7 fusion.55
  6362.3 13.9 fusion.51
  6389.3 13.7 fusion.47
  6458.9 22.2 fusion.112
  6481.1 20.7 fusion.106
  6501.8 21.7 fusion.100
  6523.5 20.7 fusion.94
  6569.7 18.8 scatter_fusion.2
  6633.1 15.7 fusion.262
  6654.9 709.4 %while.26 = (s32[]{:T(128)}, f32[1216,2,2048]{2,0,1:T(8,128)}, bf16[4,240,2048]{2,1,0:T(8,128)(2,1)}, bf16[4,240,2048]{2,1,0:T(8,128)(2,1)}, s32[1216]{0:T(1024)...) while((s32[]{:T(128)}, f32[1216,2,2048]{2,0,1:T(8,128)}, ...), condition=%wide.region_48.50_spmd.clone, body=%wide.region_46.49_spmd.clone.sunk | while | flops 6038488576 | bytes 418836544 | solution.py:369
  6711.1 17.8 multiply_reduce_fusion.9
  6728.9 17.1 multiply_convert_fusion.22
  6752.0 14.4 copy.485
  6777.8 13.5 fusion.374
  6791.3 15.9 copy.484
  6818.7 19.1 maximum_add_fusion.2
  6877.9 17.8 multiply_reduce_fusion.9
  6895.8 17.1 multiply_convert_fusion.22
  6918.8 14.4 copy.485
  6944.6 13.5 fusion.374
  6958.2 15.9 copy.484
  6985.5 23.6 maximum_add_fusion.2
  7049.2 17.8 multiply_reduce_fusion.9
  7067.1 17.1 multiply_convert_fusion.22
  7090.1 14.4 copy.485
  7129.5 15.9 copy.484
  7156.8 23.6 maximum_add_fusion.2
  7220.6 17.8 multiply_reduce_fusion.9
  7238.4 17.1 multiply_convert_fusion.22
  7261.4 14.4 copy.485
  7300.8 15.9 copy.484
  7328.1 23.6 maximum_add_fusion.2
  7410.4 19.3 scatter_custom_fusion.1
  7433.5 49.6 scatter_fusion.3
  7507.3 15.6 fusion.264
  7563.6 19.0 scatter_fusion.4
  7596.2 56.4 all-reduce.7.cloned.1.call-done
  (882 shorter events, 1114.8 us)
Async XLA Ops:
  7.2 52.8 copy-start.41
  7.2 52.2 copy-start.153
  7.2 298.2 %all-gather.27.cloned.1.call-start = ((), (), s32[]{:S(2)}) async-start(), calls=%async_computation.6 | async-start | bytes 20971520 | tf_op jit(solution)/shard_map/all_gather | solution.py:201
  7.9 496.0 %all-gather.29.cloned.1.call-start = ((), (), s32[]{:S(2)}) async-start(), calls=%async_computation.7 | async-start | bytes 10485760 | tf_op jit(solution)/shard_map/all_gather | solution.py:218
  61.8 353.4 %copy-start.9 = (bf16[448,2048]{1,0:T(8,128)(2,1)}, bf16[448,2048]{1,0:T(8,128)(2,1)S(1)}, u32[]{:S(2)}) copy-start(bf16[448,2048]{1,0:T(8,128)(2,1)S(1)} %multiply_convert_fusion.16) | copy-start | bytes 5505028
  62.4 315.8 %copy-start.130 = (f32[448,3,16]{0,2,1:T(8,128)}, f32[448,3,16]{0,2,1:T(8,128)S(1)}, u32[]{:S(2)}) copy-start(f32[448,3,16]{0,2,1:T(8,128)S(1)} %fusion.130) | copy-start | bytes 258052
  323.6 718.3 %all-gather.25.cloned.1.call-start = ((), (), s32[]{:S(2)}) async-start(), calls=%async_computation.5 | async-start | bytes 41943040 | tf_op jit(solution)/shard_map/all_gather | solution.py:202
  324.3 1278.7 %all-gather.31.cloned.1.call-start = ((), (), s32[]{:S(2)}) async-start(), calls=%async_computation.8 | async-start | bytes 41943040 | tf_op jit(solution)/shard_map/all_gather | solution.py:203
  324.9 2045.5 %all-gather.33.cloned.1.call-start = ((), (), s32[]{:S(2)}) async-start(), calls=%async_computation.12 | async-start | bytes 57671680 | tf_op jit(solution)/shard_map/all_gather | solution.py:268
  355.7 2405.4 %all-gather.35.cloned.1.call-start = ((), (), s32[]{:S(2)}) async-start(), calls=%async_computation.13 | async-start | bytes 28835840 | tf_op jit(solution)/shard_map/all_gather | solution.py:269
  373.8 3155.0 %all-gather.37.cloned.1.call-start = ((), (), s32[]{:S(2)}) async-start(), calls=%async_computation.14 | async-start | bytes 57671680 | tf_op jit(solution)/shard_map/all_gather | solution.py:268
  374.6 3545.1 %all-gather.39.cloned.1.call-start = ((), (), s32[]{:S(2)}) async-start(), calls=%async_computation.15 | async-start | bytes 28835840 | tf_op jit(solution)/shard_map/all_gather | solution.py:269
  375.3 4312.0 %all-gather.41.cloned.1.call-start = ((), (), s32[]{:S(2)}) async-start(), calls=%async_computation.16 | async-start | bytes 57671680 | tf_op jit(solution)/shard_map/all_gather | solution.py:268
  376.1 4702.0 %all-gather.43.cloned.1.call-start = ((), (), s32[]{:S(2)}) async-start(), calls=%async_computation.17 | async-start | bytes 28835840 | tf_op jit(solution)/shard_map/all_gather | solution.py:269
  376.7 5469.1 %all-gather.45.cloned.1.call-start = ((), (), s32[]{:S(2)}) async-start(), calls=%async_computation.18 | async-start | bytes 57671680 | tf_op jit(solution)/shard_map/all_gather | solution.py:268
  377.4 5859.1 %all-gather.47.cloned.1.call-start = ((), (), s32[]{:S(2)}) async-start(), calls=%async_computation.19 | async-start | bytes 28835840 | tf_op jit(solution)/shard_map/all_gather | solution.py:269
  378.0 7150.7 %reduce-scatter.16.cloned.1.call-start = ((), (), s32[]{:S(2)}) async-start(), calls=%async_computation.20 | async-start | bytes 1802240
  390.5 112.8 %copy-start.160 = (s32[4,104]{1,0:T(4,128)}, s32[4,104]{1,0:T(4,128)S(1)}, u32[]{:S(2)}) copy-start(s32[4,104]{1,0:T(4,128)S(1)} %get-tuple-element.184) | copy-start | bytes 4996
  392.7 110.6 %copy-start.148 = (s32[4,136]{1,0:T(4,128)}, s32[4,136]{1,0:T(4,128)S(1)}, u32[]{:S(2)}) copy-start(s32[4,136]{1,0:T(4,128)S(1)} %get-tuple-element.181) | copy-start | bytes 6532
  401.9 664.0 %copy-start.57 = (f32[960,16]{1,0:T(8,128)}, f32[960,16]{1,0:T(8,128)S(1)}, u32[]{:S(2)}) copy-start(f32[960,16]{1,0:T(8,128)S(1)} %gather_fusion.4) | copy-start | bytes 184324
  423.8 52.4 copy-start.65
  423.8 52.4 copy-start.79
  424.2 54.3 copy-start.128
  424.2 54.3 copy-start.138
  424.2 54.2 copy-start.158
  433.1 56.1 copy-start.29
  1073.2 198.6 %copy-start.68 = (bf16[1,6,16,2048]{3,2,1,0:T(8,128)(2,1)S(1)}, bf16[1,6,16,2048]{3,2,1,0:T(8,128)(2,1)}, u32[]{:S(2)}) copy-start(bf16[1,6,16,2048]{3,2,1,0:T(8,128)(2,1)} %copy-done.67) | copy-start | bytes 1179652
  1271.7 356.2 %copy-start.77 = (s32[1216]{0:T(1024)}, s32[1216]{0:T(1024)S(1)}, u32[]{:S(2)}) copy-start(s32[1216]{0:T(1024)S(1)} %get-tuple-element.596) | copy-start | bytes 14596
  1271.7 356.2 %copy-start.97 = (s32[1216]{0:T(1024)}, s32[1216]{0:T(1024)S(1)}, u32[]{:S(2)}) copy-start(s32[1216]{0:T(1024)S(1)} %get-tuple-element.606) | copy-start | bytes 14596
  1271.7 356.2 %copy-start.142 = (s32[4,240]{1,0:T(4,128)}, s32[4,240]{1,0:T(4,128)S(1)}, u32[]{:S(2)}) copy-start(s32[4,240]{1,0:T(4,128)S(1)} %get-tuple-element.616) | copy-start | bytes 11524
  1271.8 356.2 %copy-start.143 = (s32[4,240]{1,0:T(4,128)}, s32[4,240]{1,0:T(4,128)S(1)}, u32[]{:S(2)}) copy-start(s32[4,240]{1,0:T(4,128)S(1)} %get-tuple-element.617) | copy-start | bytes 11524
  1275.0 352.9 %copy-start.101 = (f32[4,240,16]{1,2,0:T(8,128)}, f32[4,240,16]{1,2,0:T(8,128)S(1)}, u32[]{:S(2)}) copy-start(f32[4,240,16]{1,2,0:T(8,128)S(1)} %fusion.188) | copy-start | bytes 184324
  1275.0 353.0 %copy-start.146 = (f32[4,240]{1,0:T(4,128)S(1)}, f32[4,240]{1,0:T(4,128)}, u32[]{:S(2)}) copy-start(f32[4,240]{1,0:T(4,128)} %fusion.206) | copy-start | bytes 11524
  1691.0 705.2 %copy-start.99 = (f32[240,1,2,16]{3,1,0,2:T(1,128)}, f32[240,1,2,16]{3,1,0,2:T(1,128)S(1)}, u32[]{:S(2)}) copy-start(f32[240,1,2,16]{3,1,0,2:T(1,128)S(1)} %get-tuple-element.292) | copy-start | bytes 92164
  1698.2 698.0 %copy-start.50 = (bf16[240,1,2048]{2,1,0:T(2,128)(2,1)}, bf16[240,1,2048]{2,1,0:T(2,128)(2,1)S(1)}, u32[]{:S(2)}) copy-start(bf16[240,1,2048]{2,1,0:T(2,128)(2,1)S(1)} %get-tuple-element.288) | copy-start | bytes 2949124
  2407.7 365.2 %copy-start.39 = (bf16[240,5632]{1,0:T(8,128)(2,1)}, bf16[240,5632]{1,0:T(8,128)(2,1)S(1)}, u32[]{:S(2)}) copy-start(bf16[240,5632]{1,0:T(8,128)(2,1)S(1)} %multiply_convert_fusion.14) | copy-start | bytes 8110084
  2408.5 364.4 %copy-start.106 = (f32[240,16]{0,1:T(8,128)}, f32[240,16]{0,1:T(8,128)S(1)}, u32[]{:S(2)}) copy-start(f32[240,16]{0,1:T(8,128)S(1)} %fusion.182) | copy-start | bytes 46084
  3566.9 364.5 %copy-start.33 = (bf16[240,5632]{1,0:T(8,128)(2,1)}, bf16[240,5632]{1,0:T(8,128)(2,1)S(1)}, u32[]{:S(2)}) copy-start(bf16[240,5632]{1,0:T(8,128)(2,1)S(1)} %multiply_convert_fusion.13) | copy-start | bytes 8110084
  3567.6 363.8 %copy-start.108 = (f32[240,16]{0,1:T(8,128)}, f32[240,16]{0,1:T(8,128)S(1)}, u32[]{:S(2)}) copy-start(f32[240,16]{0,1:T(8,128)S(1)} %fusion.180) | copy-start | bytes 46084
  4725.5 364.1 %copy-start.35 = (bf16[240,5632]{1,0:T(8,128)(2,1)}, bf16[240,5632]{1,0:T(8,128)(2,1)S(1)}, u32[]{:S(2)}) copy-start(bf16[240,5632]{1,0:T(8,128)(2,1)S(1)} %multiply_convert_fusion.12) | copy-start | bytes 8110084
  4726.3 363.3 %copy-start.110 = (f32[240,16]{0,1:T(8,128)}, f32[240,16]{0,1:T(8,128)S(1)}, u32[]{:S(2)}) copy-start(f32[240,16]{0,1:T(8,128)S(1)} %fusion.178) | copy-start | bytes 46084
  5884.5 362.7 %copy-start.37 = (bf16[240,5632]{1,0:T(8,128)(2,1)}, bf16[240,5632]{1,0:T(8,128)(2,1)S(1)}, u32[]{:S(2)}) copy-start(bf16[240,5632]{1,0:T(8,128)(2,1)S(1)} %multiply_convert_fusion.11) | copy-start | bytes 8110084
  5885.3 361.9 %copy-start.112 = (f32[240,16]{0,1:T(8,128)}, f32[240,16]{0,1:T(8,128)S(1)}, u32[]{:S(2)}) copy-start(f32[240,16]{0,1:T(8,128)S(1)} %fusion.176) | copy-start | bytes 46084
  6260.9 49.6 copy-start.164
  6260.9 49.6 copy-start.173
  6260.9 50.2 copy-start.20
  6331.3 88.5 %copy-start.61 = (bf16[240,1,2048]{2,1,0:T(2,128)(2,1)}, bf16[240,1,2048]{2,1,0:T(2,128)(2,1)S(1)}, u32[]{:S(2)}) copy-start(bf16[240,1,2048]{2,1,0:T(2,128)(2,1)S(1)} %get-tuple-element.285) | copy-start | bytes 2949124
  6361.6 84.1 %copy-start.116 = (f32[240,2,16]{0,2,1:T(8,128)}, f32[240,2,16]{0,2,1:T(8,128)S(1)}, u32[]{:S(2)}) copy-start(f32[240,2,16]{0,2,1:T(8,128)S(1)} %fusion.137) | copy-start | bytes 92164
  6386.4 61.6 copy-start.118
  6445.6 1085.1 %reduce-scatter.18.cloned.1.call-start = ((), (), s32[]{:S(2)}) async-start(), calls=%async_computation.21 | async-start | bytes 1802240
  6633.0 901.6 %reduce-scatter.10.cloned.1.call-start = ((), (), s32[]{:S(2)}) async-start(), calls=%async_computation.9 | async-start | bytes 10485760 | tf_op jit(solution)/shard_map/reduce_scatter | solution.py:379
  7384.6 200.7 %reduce-scatter.14.cloned.1.call-start = ((), (), s32[]{:S(2)}) async-start(), calls=%async_computation.11 | async-start | bytes 409600 | tf_op jit(solution)/shard_map/reduce_scatter | solution.py:416
  7432.0 51.1 copy-start.129
  7432.0 51.1 copy-start.139
  7432.1 51.1 copy-start.159
  7432.1 51.3 copy-start.107
  7433.5 52.5 copy-start.109
  7433.5 55.1 copy-start.111
  7433.5 57.6 copy-start.113
  7433.5 60.2 copy-start.51
  7433.5 60.2 copy-start.117
  7539.2 48.0 reduce-scatter.12.cloned.1.call-start
  7547.7 104.8 %all-reduce.7.cloned.1.call-start = ((), (), s32[]{:S(2)}) async-start(), calls=%async_computation.22 | async-start | bytes 5046272 | tf_op jit(solution)/shard_map/psum | solution.py:428
  7593.3 67.3 copy-start.1
  (162 other events, 1755.9 us)
Sparse Core Ops, SparseCore 0:
  9.6 295.7 all-gather.26
  323.7 156.9 all-gather.28
  482.3 559.5 all-gather.24
  1043.3 559.5 all-gather.30
  1604.4 765.9 all-gather.32
  2371.8 389.2 all-gather.34
  2762.7 766.0 all-gather.36
  3530.4 389.2 all-gather.38
  3921.3 766.0 all-gather.40
  4688.8 389.2 all-gather.42
  5079.7 766.0 all-gather.44
  5847.2 389.2 all-gather.46
  6445.7 31.5 reduce-scatter.15
  6633.1 31.5 reduce-scatter.17
  7384.7 142.7 reduce-scatter.9
  7539.3 18.3 reduce-scatter.13
  7560.4 18.8 reduce-scatter.11
  7589.4 63.1 all-reduce.6
where the time goes:
time: 7680 us; the launch traced here: 7670 us
  waiting for transfers between devices  5490 us (71%)
  matrix products  884 us (12%)
  local copies, waits for them, and re-layouts  661 us (9%)
  other arithmetic  492 us (6%)
  blocking collectives  88.6 us (1%)
    all_gather x4, waiting for transfers between devices, fetch_expert(): lax.all_gather(w_gate_up[expert], 'shard', axis=2, tiled=True)  2930 us
    all_gather x4, waiting for transfers between devices, fetch_expert(): lax.all_gather(w_down[expert], 'shard', axis=0, tiled=True)  1410 us
    all_gather x1, waiting for transfers between devices, on_device(): lax.all_gather(w_query, 'shard', axis=2, tiled=True)  528 us
    all_gather x1, waiting for transfers between devices, on_device(): lax.all_gather(w_out, 'shard', axis=2, tiled=True)  328 us
    all_gather x1, waiting for transfers between devices, on_device(): lax.all_gather(w_kv, 'shard', axis=2, tiled=True)  238 us
    while x108, local copies, waits for them, and re-layouts  161 us
  transfers between devices with their start and end apart: 18, of which 12 were waited for; matrix products, arithmetic and copies ran while one was open for 23% of the time, Pallas kernels for 0%

commit v1 on v0

v1 whole, which is shorter than its diff:
```python
import jax
import jax.numpy as jnp
from jax import lax
from jax.sharding import PartitionSpec as P

HD = 128
EPSILON = 1e-05
HIGHEST = lax.Precision.HIGHEST
NEG_FILL = -1e30
F32 = jnp.float32
BF16 = jnp.bfloat16


def dot32(former, latter):
    return jnp.dot(former, latter, preferred_element_type=F32)


def exact_mm(former, latter):
    return jnp.dot(former, latter, precision=HIGHEST)


def norm_rows(values, scaling):
    inverse = lax.rsqrt(jnp.mean(values * values, axis=-1, keepdims=True) + EPSILON)
    return (values * inverse * scaling, inverse)


def norm_back(values, inverse, scaling, upstream):
    weighted = upstream * scaling
    inner_mean = jnp.mean(weighted * values, axis=-1, keepdims=True)
    return inverse * weighted - values * (inverse * inverse * inverse) * inner_mean


def capacity(block_rows, experts, top_count):
    return min(block_rows, ((block_rows * top_count + experts - 1) // experts + 7) // 8 * 8 + 8)


def hits(routes, experts):
    labels = jnp.arange(experts, dtype=jnp.int32)
    return (routes[:, :, None] == labels[None, None, :]).astype(F32)


def slot_onehots(routes, experts, block):
    rows, top_count = routes.shape
    blocks = rows // block
    slot_cap = capacity(block, experts, top_count)
    member = jnp.sum(hits(routes, experts), axis=1).reshape(blocks, block, experts)
    place = jnp.arange(block, dtype=jnp.int32)
    before = (place[None, :] < place[:, None]).astype(BF16)
    ranked = jnp.einsum("rq,bqe->ber", before, member.astype(BF16), preferred_element_type=F32)
    slots = jnp.arange(slot_cap, dtype=F32)
    matched = (ranked[:, :, None, :] == slots[None, None, :, None]) & (
        member.transpose(0, 2, 1)[:, :, None, :] > 0
    )
    return matched.astype(BF16)


def route_shares(logits, routes):
    chosen = jnp.einsum("rte,re->rt", hits(routes, logits.shape[1]), logits, precision=HIGHEST)
    return jax.nn.softmax(chosen, axis=-1)


def shares_back(shares, routes, experts, d_shares):
    d_chosen = shares * (d_shares - jnp.sum(shares * d_shares, axis=-1, keepdims=True))
    return jnp.sum(d_chosen[:, :, None] * hits(routes, experts), axis=1)


def pick_expert(per_expert, routes):
    out = []
    for t in range(routes.shape[1]):
        total = per_expert[0]
        for e in range(1, per_expert.shape[0]):
            total = jnp.where(routes[:, t, None] == e, per_expert[e], total)
        out.append(total)
    return jnp.stack(out)


def spread_expert(per_choice, routes, experts):
    out = []
    for e in range(experts):
        total = jnp.zeros(per_choice.shape[1:], per_choice.dtype)
        for t in range(routes.shape[1]):
            total = jnp.where(routes[:, t, None] == e, per_choice[t], total)
        out.append(total)
    return jnp.concatenate(out, axis=1)


def heads_of(values):
    return values.reshape(values.shape[:-1] + (values.shape[-1] // HD, HD))


def attend_prompt(q, k, v):
    tops, rows, _ = q.shape
    s = jnp.einsum("tqhd,khd->htqk", heads_of(q), heads_of(k), preferred_element_type=F32)
    place = jnp.arange(rows)
    s = jnp.where(place[None, :] <= place[:, None], s * HD**-0.5, NEG_FILL)
    top = jnp.max(s, axis=-1, keepdims=True)
    p = jnp.exp(s - top)
    total = jnp.sum(p, axis=-1, keepdims=True)
    o = jnp.einsum("htqk,khd->tqhd", (p / total).astype(BF16), heads_of(v), preferred_element_type=F32)
    return o.reshape(q.shape).astype(BF16), top + jnp.log(total)


def attend_prompt_back(q, k, v, do, lse):
    rows = q.shape[1]
    qh, kh, vh, gh = (heads_of(m) for m in (q, k, v, do))
    place = jnp.arange(rows)
    s = jnp.einsum("tqhd,khd->htqk", qh, kh, preferred_element_type=F32) * HD**-0.5
    p = jnp.where(place[None, :] <= place[:, None], jnp.exp(s - lse), 0.0)
    dp = jnp.einsum("tqhd,khd->htqk", gh, vh, preferred_element_type=F32)
    ds = (p * (dp - jnp.sum(p * dp, axis=-1, keepdims=True))).astype(BF16)
    dq = jnp.einsum("htqk,khd->tqhd", ds, kh, preferred_element_type=F32) * HD**-0.5
    dk = jnp.einsum("htqk,tqhd->khd", ds, qh, preferred_element_type=F32) * HD**-0.5
    dv = jnp.einsum("htqk,tqhd->khd", p.astype(BF16), gh, preferred_element_type=F32)
    return dq.reshape(q.shape).astype(BF16), dk.reshape(k.shape), dv.reshape(k.shape)


def cont_scores(qh, kph, kch, length):
    s_p = jnp.einsum("tcqhd,khd->htcqk", qh, kph, preferred_element_type=F32) * HD**-0.5
    s_c = jnp.einsum("tcqhd,ckhd->htcqk", qh, kch, preferred_element_type=F32) * HD**-0.5
    place = jnp.arange(length)
    s_c = jnp.where(place[None, :] <= place[:, None], s_c, NEG_FILL)
    return s_p, s_c


def attend_cont(q, kp, vp, kc, vc, length):
    tops, rows, width = q.shape
    conts = rows // length
    qh = heads_of(q.reshape(tops, conts, length, width))
    kch = heads_of(kc.reshape(conts, length, width))
    vch = heads_of(vc.reshape(conts, length, width))
    s_p, s_c = cont_scores(qh, heads_of(kp), kch, length)
    top = jnp.maximum(jnp.max(s_p, axis=-1, keepdims=True), jnp.max(s_c, axis=-1, keepdims=True))
    p_p, p_c = jnp.exp(s_p - top), jnp.exp(s_c - top)
    total = jnp.sum(p_p, axis=-1, keepdims=True) + jnp.sum(p_c, axis=-1, keepdims=True)
    o = jnp.einsum(
        "htcqk,khd->tcqhd", (p_p / total).astype(BF16), heads_of(vp), preferred_element_type=F32
    ) + jnp.einsum("htcqk,ckhd->tcqhd", (p_c / total).astype(BF16), vch, preferred_element_type=F32)
    return o.reshape(q.shape).astype(BF16), top + jnp.log(total)


def attend_cont_back(q, kp, vp, kc, vc, do, lse, length):
    tops, rows, width = q.shape
    conts = rows // length
    qh = heads_of(q.reshape(tops, conts, length, width))
    gh = heads_of(do.reshape(tops, conts, length, width))
    kch = heads_of(kc.reshape(conts, length, width))
    vch = heads_of(vc.reshape(conts, length, width))
    kph, vph = heads_of(kp), heads_of(vp)
    s_p, s_c = cont_scores(qh, kph, kch, length)
    p_p, p_c = jnp.exp(s_p - lse), jnp.exp(s_c - lse)
    dp_p = jnp.einsum("tcqhd,khd->htcqk", gh, vph, preferred_element_type=F32)
    dp_c = jnp.einsum("tcqhd,ckhd->htcqk", gh, vch, preferred_element_type=F32)
    delta = jnp.sum(p_p * dp_p, axis=-1, keepdims=True) + jnp.sum(p_c * dp_c, axis=-1, keepdims=True)
    ds_p = (p_p * (dp_p - delta)).astype(BF16)
    ds_c = (p_c * (dp_c - delta)).astype(BF16)
    dq = jnp.einsum("htcqk,khd->tcqhd", ds_p, kph, preferred_element_type=F32) + jnp.einsum(
        "htcqk,ckhd->tcqhd", ds_c, kch, preferred_element_type=F32
    )
    dkp = jnp.einsum("htcqk,tcqhd->khd", ds_p, qh, preferred_element_type=F32) * HD**-0.5
    dkc = jnp.einsum("htcqk,tcqhd->ckhd", ds_c, qh, preferred_element_type=F32) * HD**-0.5
    dvp = jnp.einsum("htcqk,tcqhd->khd", p_p.astype(BF16), gh, preferred_element_type=F32)
    dvc = jnp.einsum("htcqk,tcqhd->ckhd", p_c.astype(BF16), gh, preferred_element_type=F32)
    flat = lambda m: m.reshape(-1, width)
    return (dq * HD**-0.5).reshape(q.shape).astype(BF16), flat(dkp), flat(dvp), flat(dkc), flat(dvc)


def on_device(
    prompt_in,
    cont_in,
    cotan_prompt,
    cotan_cont,
    routes_attn_p,
    routes_attn_c,
    routes_ffn_p,
    routes_ffn_c,
    adapter_pick,
    norm_gains,
    router_attn,
    router_ffn,
    w_kv,
    w_query,
    w_out,
    w_gate_up,
    w_down,
    ada_in,
    ada_out,
    ada_down,
    ada_ffn,
):
    features = prompt_in.shape[2]
    n_attn = w_query.shape[0]
    n_ffn = w_down.shape[0]
    shards = lax.axis_size("shard")
    reps = lax.axis_size("rep")
    rep_id = lax.axis_index("rep")
    cont_len = cont_in.shape[2]
    sizes = (prompt_in.shape[1], cont_in.shape[1] * cont_len)
    width = w_kv.shape[2]
    both = range(2)

    def gather(values):
        return lax.all_gather(values, "shard", axis=0, tiled=True)

    def scatter(values):
        return lax.psum_scatter(values, "shard", scatter_dimension=0, tiled=True)

    flat = lambda m: m[0].reshape(-1, m.shape[-1])
    x_own = [flat(prompt_in), flat(cont_in)]
    c_own = [flat(cotan_prompt), flat(cotan_cont)]
    ra_own = [flat(routes_attn_p), flat(routes_attn_c)]
    rf_own = [flat(routes_ffn_p), flat(routes_ffn_c)]
    chosen = adapter_pick[0]
    own_in = lax.dynamic_index_in_dim(ada_in, chosen, 0, keepdims=False)
    own_out = lax.dynamic_index_in_dim(ada_out, chosen, 0, keepdims=False)
    own_down = lax.dynamic_index_in_dim(ada_down, chosen, 0, keepdims=False)
    own_ffn = lax.dynamic_index_in_dim(ada_ffn, chosen, 0, keepdims=False)
    gain_one = norm_gains[0].astype(F32)
    gain_two = norm_gains[1].astype(F32)

    x_all = [gather(m) for m in x_own]
    routes_own = jnp.concatenate(
        [jnp.concatenate([ra_own[i], rf_own[i]], axis=1) for i in both], axis=0
    )
    routes_all = lax.all_gather(routes_own, "shard", axis=0)
    tops = ra_own[0].shape[1]
    part = [routes_all[:, : sizes[0]], routes_all[:, sizes[0] :]]
    part = [m.reshape(-1, 2 * tops) for m in part]
    ra = [m[:, :tops] for m in part]
    rf = [m[:, tops:] for m in part]
    factors = lax.all_gather(
        jnp.concatenate([own_in[:3], own_in[4:6], own_out[3:5]], axis=0), "shard", axis=2, tiled=True
    )
    a_qkv, a_ff, b_o, b_down = factors[:3], factors[3:5], factors[5], factors[6]
    b_qkv, a_o = own_out[:3], own_in[3]
    piece = width // reps
    mine = lax.dynamic_index_in_dim(
        w_out.reshape(n_attn, shards, reps, piece, w_out.shape[2]), rep_id, 2, keepdims=False
    )
    turned = lax.all_to_all(mine, "shard", 1, 3, tiled=True).reshape(n_attn, piece, features)
    w_o = lax.all_gather(turned, "rep", axis=1, tiled=True)
    c_all = [gather(m) for m in c_own]

    n1, wa, low1, q, k, v = [], [], [], [], [], []
    for i in both:
        normed, _ = norm_rows(x_all[i].astype(F32), gain_one)
        normed = normed.astype(BF16)
        n1.append(normed)
        wa.append(route_shares(dot32(normed, router_attn), ra[i]))
        low = jnp.einsum("nd,jrd->jnr", normed, a_qkv, preferred_element_type=F32)
        low1.append(low)
        shift = exact_mm(low[0], b_qkv[0].astype(F32))
        per_expert = jnp.einsum("nd,edk->enk", normed, w_query, preferred_element_type=F32) + shift
        q.append(pick_expert(per_expert, ra[i]).astype(BF16))
        k.append((dot32(normed, w_kv[0]) + exact_mm(low[1], b_qkv[1].astype(F32))).astype(BF16))
        v.append((dot32(normed, w_kv[1]) + exact_mm(low[2], b_qkv[2].astype(F32))).astype(BF16))
    o, lse = [None, None], [None, None]
    o[0], lse[0] = attend_prompt(q[0], k[0], v[0])
    o[1], lse[1] = attend_cont(q[1], k[0], v[0], k[1], v[1], cont_len)
    w_o_flat = w_o.reshape(n_attn * width, features)
    h1, n2_own, r2, o_sum, low_o = [], [], [], [], []
    for i in both:
        weighted = o[i].astype(F32) * wa[i].T[:, :, None]
        total = jnp.sum(weighted, axis=0)
        low = exact_mm(total, a_o.astype(F32).T)
        o_sum.append(total)
        low_o.append(low)
        partial = dot32(spread_expert(weighted.astype(BF16), ra[i], n_attn), w_o_flat) + exact_mm(
            low, b_o.astype(F32)
        )
        hidden = x_own[i].astype(F32) + scatter(partial.astype(BF16)).astype(F32)
        normed, inverse = norm_rows(hidden, gain_two)
        h1.append(hidden)
        r2.append(inverse)
        n2_own.append(normed.astype(BF16))

    n2 = [gather(m) for m in n2_own]
    outs, dh1 = [], []
    g_a_ff = jnp.zeros(a_ff.shape, F32)
    g_c_ff = jnp.zeros(own_ffn.shape, F32)
    g_b_down = jnp.zeros(b_down.shape, F32)
    g_a_down = jnp.zeros(own_down.shape, F32)
    for i in both:
        hot = slot_onehots(rf[i], n_ffn, sizes[i])
        wf = route_shares(dot32(n2[i], router_ffn), rf[i])
        wf_rows = jnp.sum(wf[:, :, None] * hits(rf[i], n_ffn), axis=1).reshape(shards, sizes[i], n_ffn)
        wf_slots = jnp.einsum("besr,bre->ebs", hot.astype(F32), wf_rows, precision=HIGHEST)
        blocks = lambda m: m.reshape(shards, sizes[i], m.shape[-1])
        to_slots = lambda m: jnp.einsum(
            "besr,brd->ebsd", hot, blocks(m), preferred_element_type=F32
        ).astype(BF16).reshape(n_ffn, -1, m.shape[-1])
        to_rows = lambda m: jnp.einsum(
            "besr,ebsd->brd", hot, m.reshape(n_ffn, shards, -1, m.shape[-1]), preferred_element_type=F32
        ).reshape(-1, m.shape[-1])
        xs, cs = to_slots(n2[i]), to_slots(c_all[i])
        wf_slots = wf_slots.reshape(n_ffn, -1)
        y_parts, d_parts, dw_parts = [], [], []
        for e in range(n_ffn):
            low = [dot32(xs[e], a_ff[j].T) for j in both]
            g = [dot32(xs[e], w_gate_up[e, j]) + exact_mm(low[j], own_ffn[j].astype(F32)) for j in both]
            sig = jax.nn.sigmoid(g[0])
            act = (g[0] * sig * g[1]).astype(BF16)
            low_down = dot32(act, own_down.T)
            y = dot32(act, w_down[e]) + exact_mm(low_down, b_down.astype(F32))
            ws = wf_slots[e][:, None]
            c_low = dot32(cs[e], b_down.T)
            d_act = dot32(cs[e], w_down[e].T) + exact_mm(c_low, own_down.astype(F32))
            dw_parts.append(jnp.sum(d_act * act.astype(F32), axis=-1, keepdims=True))
            d_act = d_act * ws
            dg = [
                (d_act * g[1] * sig * (1.0 + g[0] * (1.0 - sig))).astype(BF16),
                (d_act * g[0] * sig).astype(BF16),
            ]
            d_low = [dot32(dg[j], own_ffn[j].T) for j in both]
            dx = sum(
                dot32(dg[j], w_gate_up[e, j].T) + exact_mm(d_low[j], a_ff[j].astype(F32)) for j in both
            )
            y_parts.append((ws * y).astype(BF16))
            d_parts.append(dx.astype(BF16))
            g_b_down = g_b_down + dot32((ws * low_down).astype(BF16).T, cs[e])
            g_a_down = g_a_down + dot32((ws * c_low).astype(BF16).T, act)
            g_c_ff = g_c_ff + jnp.stack([dot32(low[j].astype(BF16).T, dg[j]) for j in both])
            g_a_ff = g_a_ff + jnp.stack([dot32(d_low[j].astype(BF16).T, xs[e]) for j in both])
        y_rows = scatter(to_rows(jnp.stack(y_parts)).astype(BF16)).astype(F32)
        outs.append((h1[i] + y_rows).astype(BF16))
        d_rows = scatter(to_rows(jnp.stack(d_parts)).astype(BF16)).astype(F32)
        dw = jnp.stack(dw_parts).reshape(n_ffn, shards, -1)
        dw_rows = jnp.einsum("besr,ebs->bre", hot.astype(F32), dw, precision=HIGHEST)
        dw_rows = scatter(dw_rows.reshape(-1, n_ffn))
        wf_own = route_shares(dot32(n2_own[i], router_ffn), rf_own[i])
        dw_top = jnp.einsum("rte,re->rt", hits(rf_own[i], n_ffn), dw_rows, precision=HIGHEST)
        d_logits = shares_back(wf_own, rf_own[i], n_ffn, dw_top)
        d_rows = d_rows + exact_mm(d_logits, router_ffn.astype(F32).T)
        dh1.append(c_own[i].astype(F32) + norm_back(h1[i], r2[i], gain_two, d_rows))

    dh1_all = [gather(m.astype(BF16)) for m in dh1]
    g_a_o = jnp.zeros(a_o.shape, F32)
    g_b_o = jnp.zeros(b_o.shape, F32)
    do, dwa = [], []
    for i in both:
        d_low = dot32(dh1_all[i], b_o.T)
        per_expert = jnp.einsum("nd,ekd->enk", dh1_all[i], w_o, preferred_element_type=F32)
        per_expert = per_expert + exact_mm(d_low, a_o.astype(F32))
        picked = pick_expert(per_expert, ra[i])
        dwa.append(jnp.sum(picked * o[i].astype(F32), axis=-1).T)
        do.append((picked * wa[i].T[:, :, None]).astype(BF16))
        g_a_o = g_a_o + dot32(d_low.astype(BF16).T, o_sum[i].astype(BF16))
        g_b_o = g_b_o + dot32(low_o[i].astype(BF16).T, dh1_all[i])
    dq, dk, dv = [None, None], [None, None], [None, None]
    dq[0], dk[0], dv[0] = attend_prompt_back(q[0], k[0], v[0], do[0], lse[0])
    dq[1], dkp, dvp, dk[1], dv[1] = attend_cont_back(
        q[1], k[0], v[0], k[1], v[1], do[1], lse[1], cont_len
    )
    dk[0], dv[0] = dk[0] + dkp, dv[0] + dvp
    g_a_qkv = jnp.zeros(a_qkv.shape, F32)
    g_b_qkv = jnp.zeros(b_qkv.shape, F32)
    grads = []
    for i in both:
        dq_sum = jnp.sum(dq[i].astype(F32), axis=0).astype(BF16)
        dkv = [dk[i].astype(BF16), dv[i].astype(BF16)]
        d_mats = [dq_sum] + dkv
        d_low = [dot32(d_mats[j], b_qkv[j].T) for j in range(3)]
        d_rows = jnp.einsum(
            "nek,edk->nd",
            spread_expert(dq[i], ra[i], n_attn).reshape(-1, n_attn, width),
            w_query,
            preferred_element_type=F32,
        )
        d_rows = d_rows + dot32(dkv[0], w_kv[0].T) + dot32(dkv[1], w_kv[1].T)
        d_rows = d_rows + sum(exact_mm(d_low[j], a_qkv[j].astype(F32)) for j in range(3))
        g_a_qkv = g_a_qkv + jnp.stack([dot32(d_low[j].astype(BF16).T, n1[i]) for j in range(3)])
        g_b_qkv = g_b_qkv + jnp.stack(
            [dot32(low1[i][j].astype(BF16).T, d_mats[j]) for j in range(3)]
        )
        d_rows = scatter(d_rows.astype(BF16)).astype(F32)
        dw_top = scatter(dwa[i])
        x32 = x_own[i].astype(F32)
        normed, inverse = norm_rows(x32, gain_one)
        wa_own = route_shares(dot32(normed.astype(BF16), router_attn), ra_own[i])
        d_logits = shares_back(wa_own, ra_own[i], n_attn, dw_top)
        d_rows = d_rows + exact_mm(d_logits, router_attn.astype(F32).T)
        grads.append(dh1[i] + norm_back(x32, inverse, gain_one, d_rows))

    parts = jnp.concatenate([g_a_qkv, g_a_ff, g_b_o[None], g_b_down[None]], axis=0)
    parts = lax.psum_scatter(parts.astype(BF16), "shard", scatter_dimension=2, tiled=True).astype(F32)
    g_in = jnp.concatenate([parts[:3], g_a_o[None], parts[3:5]], axis=0)
    g_out = jnp.concatenate([g_b_qkv, parts[5:7]], axis=0)
    slot_hot = (jnp.arange(ada_in.shape[0], dtype=jnp.int32) == chosen).astype(F32)

    def over_groups(grad):
        spread = slot_hot.reshape((-1,) + (1,) * grad.ndim) * grad[None]
        return lax.psum(spread.astype(BF16), "rep").astype(F32)

    shape_c = (1,) + cont_in.shape[1:]
    return (
        outs[0][None],
        outs[1].reshape(shape_c),
        grads[0][None],
        grads[1].reshape(shape_c),
        over_groups(g_in),
        over_groups(g_out),
        over_groups(g_a_down),
        over_groups(g_c_ff),
    )


def solution(mesh):
    rows = (P("rep", "shard", None), P("rep", "shard", None, None))
    last = (
        P(None, None, None, "shard"),
        P(None, None, None, "shard"),
        P(None, None, "shard"),
        P(None, None, None, "shard"),
    )
    in_specs = (
        rows * 4
        + (P("rep"), P(), P(), P())
        + (P(None, None, "shard"),) * 3
        + (P(None, None, None, "shard"), P(None, "shard", None))
        + last
    )
    return jax.shard_map(
        on_device, mesh=mesh, in_specs=in_specs, out_specs=rows * 2 + last, check_vma=False
    )
```

time: 7680 us -> 1910 us (0.25)
  waiting for transfers between devices: 5490 us -> 463 us
  local copies, waits for them, and re-layouts: 661 us -> 115 us
  other arithmetic: 492 us -> 186 us
  matrix products: 884 us -> 1030 us
    all_gather x12 -> x9, waiting for transfers between devices: 5430 us -> 157 us  [the longest x8 157 us: gather(): return lax.all_gather(values, 'shard', axis=0, tiled=True)]
    reduce_scatter x3 -> x9, waiting for transfers between devices: 0.02 us -> 260 us  [the longest x8 260 us: scatter(): return lax.psum_scatter(values, 'shard', scatter_dimension=0, tiled=True)]
    scatter-add x6 -> x0, other arithmetic: 175 us -> none  [the longest x1 49.6 us: on_device(): d_shares_a = jnp.zeros(shares_attn.shape, jnp.float32).at[source_a.reshap...]
    dot_general x18 -> x70, matrix products: 69.1 us -> 242 us  [exact_mm(): return jnp.dot(former, latter, precision=HIGHEST)]
    while x108 -> x0, local copies, waits for them, and re-layouts: 161 us -> none
    gather x28 -> x0, local copies, waits for them, and re-layouts: 106 us -> none  [the longest x2 21.5 us: on_device(): up_slots = upstream[source_f]]
    reshape x16 -> x4, local copies, waits for them, and re-layouts: 102 us -> 3.4 us  [the longest x1 2.59 us: on_device(): lax.all_to_all(mine, 'shard', 1, 3, tiled=True)]
    add x10 -> x6, other arithmetic: 97.3 us -> 6.22 us  [the longest x1 4.86 us: on_device(): grads.append(dh1[i] + norm_back(x32, inverse, gain_one, d_rows))]
  transfers between devices with their start and end apart: 18 -> 24, of which waited for: 12 -> 11; matrix products, arithmetic and copies ran while one was open for 23% -> 56% of each run, Pallas kernels for 0% -> 0%
where the time goes in v1:
time: 1910 us; the launch traced here: 1900 us
  matrix products  1030 us (54%)
  waiting for transfers between devices  463 us (24%)
  other arithmetic  186 us (10%)
  local copies, waits for them, and re-layouts  115 us (6%)
  blocking collectives  77.7 us (4%)
  between operations  20.1 us (1%)
    dot_general x184, matrix products, dot32(): return jnp.dot(former, latter, preferred_element_type=F32)  490 us
    reduce_scatter x8, waiting for transfers between devices, scatter(): return lax.psum_scatter(values, 'shard', scatter_dimension=0, tiled=True)  260 us
    dot_general x70, matrix products, exact_mm(): return jnp.dot(former, latter, precision=HIGHEST)  242 us
    all_gather x8, waiting for transfers between devices, gather(): return lax.all_gather(values, 'shard', axis=0, tiled=True)  157 us
    all_gather x1, blocking collectives, on_device(): routes_all = lax.all_gather(routes_own, 'shard', axis=0)  57.6 us
    psum x1, waiting for transfers between devices, over_groups(): return lax.psum(spread.astype(BF16), 'rep').astype(F32)  43.4 us
    unnamed x882, local copies, waits for them, and re-layouts  42.8 us
  transfers between devices with their start and end apart: 24, of which 11 were waited for; matrix products, arithmetic and copies ran while one was open for 56% of the time, Pallas kernels for 0%

profile of v1, /device:TPU:0, one launch (start us, length us, event | category | flops | bytes accessed | tf_op | source)
XLA Modules:
  0.0 1896.1 jit_solution(4762209896098107672)
XLA Ops:
  17.7 57.6 %all-gather.3 = s32[4,448,4]{1,2,0:T(4,128)S(1)} all-gather(s32[1,448,4]{1,2,0:T(4,128)S(1)} %add_bitcast_fusion.2), channel_id=2, replica_groups=mesh['rep'=8,'shard'=4] {'shard'}, dimensions={0}, use_global_device_ids=true | all-gather | bytes 35840 | tf_op jit(solution)/shard_map/all_gather | solution.py:224
  81.7 20.2 %all_gather.39 = bf16[7,16,2048]{2,1,0:T(8,128)(2,1)S(1)} all-gather(bf16[7,16,512]{2,1,0:T(8,128)(2,1)S(1)} %pad_maximum_fusion.7), channel_id=1, replica_groups=mesh['rep'=8,'shard'=4] {'shard'}, dimensions={2}, use_global_device_ids=true | all-gather | bytes 573440 | tf_op jit(solution)/shard_map/all_gather | solution.py:230
  121.0 11.5 fusion.385
  134.5 10.2 add_bitcast_fusion.1
  166.8 16.8 all-gather.28.cloned.1.call-done
  191.4 14.5 fusion.376
  208.2 13.0 add_bitcast_fusion
  233.5 10.2 multiply_reduce_fusion.2
  244.5 11.8 fusion.1
  262.4 12.2 multiply_reduce_fusion.6
  292.7 14.2 select_reduce_fusion
  306.9 14.3 fusion
  321.3 9.7 fusion.234
  336.7 19.1 %multiply_reduce_fusion.4 = (f32[1024,4,128]{0,2,1:T(8,128)}, bf16[4,128,2,1024]{3,1,2,0:T(8,128)(2,1)}) fusion(f32[2,1024]{1,0:T(2,128)S(1)} %divide_bitcast_fusion, bf16[1024,4,128,1]{0,2,3,1:T(8,128)(2,1)S(1)} %bitcast.1350, f32[4,2,1024,1024]{2,3,1,0:T(8,128)} %get-tuple-element.157, f32[4,2,1024]{2,1,0:T(2,128)S(1)} %fusion, ...), kind=kOutput, calls=%fused_computation.226 | convolution fusion | flops 2193096704 | bytes 39919616 | tf_op jit(solution)/shard_map/htqk,khd->tqhd/dot_general | solution.py:99
  363.7 8.9 fusion.157
  378.1 16.4 reduce-scatter.26.cloned.1.call-done
  400.2 73.2 %reduce-scatter.22.cloned.1.call-done = bf16[256,2048]{1,0:T(8,128)(2,1)} async-done(((bf16[1024,2048]{1,0:T(8,128)(2,1)}), bf16[256,2048]{1,0:T(8,128)(2,1)}) %reduce-scatter.22.cloned.1.call-update) | async-done | bytes 1048592 | tf_op jit(solution)/shard_map/reduce_scatter | solution.py:205
  475.7 63.9 %all-gather.20.cloned.1.call-done = bf16[768,2048]{1,0:T(8,128)(2,1)} async-done(((bf16[192,2048]{1,0:T(8,128)(2,1)}), bf16[768,2048]{1,0:T(8,128)(2,1)}) %all-gather.20.cloned.1.call-update) | async-done | bytes 3145744 | tf_op jit(solution)/shard_map/all_gather | solution.py:202
  574.2 6.9 fusion.149
  588.0 7.3 fusion.101
  615.7 8.1 fusion.57
  775.1 14.0 all-gather.16.cloned.1.call-done
  792.9 8.1 convert_bitcast_fusion.1
  814.6 8.0 fusion.71
  822.6 7.9 fusion.79
  830.5 8.0 fusion.143
  838.5 8.0 fusion.151
  846.5 8.0 fusion.95
  854.5 7.9 fusion.103
  862.4 7.8 fusion.119
  870.3 7.9 fusion.127
  886.3 9.0 fusion.59
  896.7 8.0 fusion.131
  906.0 8.0 fusion.83
  915.3 8.3 fusion.107
  1029.2 8.2 fusion.139
  1037.3 8.0 fusion.147
  1045.4 8.0 fusion.91
  1053.4 8.0 fusion.99
  1061.5 8.0 fusion.115
  1069.5 7.9 fusion.123
  1077.6 8.7 add_convert_fusion.4
  1091.6 7.3 add_convert_fusion.3
  1098.9 7.3 add_convert_fusion.5
  1132.6 29.9 %all-gather.26.cloned.1.call-done = bf16[768,2048]{1,0:T(8,128)(2,1)} async-done(((bf16[192,2048]{1,0:T(8,128)(2,1)}), bf16[768,2048]{1,0:T(8,128)(2,1)}) %all-gather.26.cloned.1.call-update) | async-done | bytes 3145744 | tf_op jit(solution)/shard_map/all_gather | solution.py:202
  1167.1 9.4 bitcast_add_fusion.3
  1192.5 18.3 multiply_reduce_fusion.1
  1217.9 22.3 %reduce-scatter.30.cloned.1.call-done = bf16[256,2048]{1,0:T(8,128)(2,1)} async-done(((bf16[1024,2048]{1,0:T(8,128)(2,1)}), bf16[256,2048]{1,0:T(8,128)(2,1)}) %reduce-scatter.30.cloned.1.call-update) | async-done | bytes 1048592 | tf_op jit(solution)/shard_map/reduce_scatter | solution.py:205
  1249.8 23.2 %multiply_convert_fusion.1 = (bf16[4,2,8,96,1024]{4,3,2,1,0:T(8,128)(2,1)S(1)}, bf16[4,2,8,96,1024]{4,3,2,1,0:T(8,128)(2,1)}) fusion(f32[4,2,8,96,1024]{4,3,2,1,0:T(8,128)} %get-tuple-element.170, f32[4,2,8,96,1024]{4,3,2,1,0:T(8,128)} %get-tuple-element.162, f32[4,2,8,96]{3,2,1,0:T(8,128)S(1)} %copy_add_fusion, f32[4,2,8,96]{3,2,1,0:T(8,128)S(1)} %copy-done.202), kind=kLoop, calls=%fused_computation.7 | loop fusion | flops 37748736 | bytes 75546624 | tf_op jit(solution)/shard_map/convert_element_type | solution.py:154
  1295.7 32.6 %all-gather.22.cloned.1.call-done = bf16[1024,2048]{1,0:T(8,128)(2,1)} async-done(((bf16[256,2048]{1,0:T(8,128)(2,1)}), bf16[1024,2048]{1,0:T(8,128)(2,1)}) %all-gather.22.cloned.1.call-update) | async-done | bytes 4194320 | tf_op jit(solution)/shard_map/all_gather | solution.py:202
  1333.6 11.5 bitcast_add_fusion.1
  1348.2 16.7 fusion.3
  1364.9 25.2 %multiply_reduce_fusion = (f32[4,2,1024]{2,1,0:T(2,128)S(1)}, f32[4,2,1024,1024]{2,3,1,0:T(8,128)}) fusion(f32[4,2,1024,1024]{2,3,1,0:T(8,128)} %get-tuple-element.157, f32[4,2,1024]{2,1,0:T(2,128)S(1)} %bitcast.1407, pred[1024,1024]{0,1:T(8,128)(4,1)S(1)} %copy-done.14, bf16[1024,4,128,1]{0,2,3,1:T(8,128)(2,1)} %bitcast.1349, ...), kind=kOutput, calls=%fused_computation.1 | convolution fusion | flops 2192564224 | bytes 73474048 | tf_op jit(solution)/shard_map/tqhd,khd->htqk/dot_general | solution.py:109
  1390.1 28.7 %multiply_convert_fusion = bf16[4,2,1024,1024]{2,3,1,0:T(8,128)(2,1)} fusion(f32[4,2,1024,1024]{2,3,1,0:T(8,128)} %get-tuple-element.174, f32[4,2,1024,1024]{2,3,1,0:T(8,128)} %get-tuple-element.157, f32[4,2,1024]{2,1,0:T(2,128)S(1)} %get-tuple-element.173, f32[4,2,1024]{2,1,0:T(2,128)S(1)} %bitcast.1408, pred[1024,1024]{0,1:T(8,128)(4,1)S(1)} %copy-done.14), kind=kLoop, calls=%fused_computation | loop fusion | flops 50331648 | bytes 85000192 | tf_op jit(solution)/shard_map/convert_element_type | solution.py:110
  1418.8 13.5 fusion.349
  1432.3 11.3 fusion.691
  1443.5 7.7 fusion.289
  1490.4 11.0 fusion.242
  1501.4 9.9 fusion.56
  1597.6 13.4 fusion.165
  1614.9 18.0 fusion.34
  1681.6 43.4 %all-reduce.3.cloned.1.call-done = (bf16[8,6,16,512]{3,2,1,0:T(8,128)(2,1)}, bf16[8,5,16,512]{3,2,1,0:T(8,128)(2,1)}, bf16[8,16,1408]{2,1,0:T(8,128)(2,1)}, bf16[8,2,16,1408]{3,2,1,0:T(8,128)(2,1)}) async-done(((bf16[8,6,16,512]{3,2,1,0:T(8,128)(2,1)}, bf16[8,5,16,512]{3,2,1,0:T(8,128)(2,1)}, bf16[8,16,1408]{2,1,0:T(8,128)(2,1)}, bf16[8,2,16,1408]{3,2,1,0:T(8,128)(2,1)}), ...) | async-done | bytes 2523152 | tf_op jit(solution)/shard_map/psum | solution.py:391
  1732.0 71.7 %reduce-scatter.34.cloned.1.call-done = bf16[256,2048]{1,0:T(8,128)(2,1)} async-done(((bf16[1024,2048]{1,0:T(8,128)(2,1)}), bf16[256,2048]{1,0:T(8,128)(2,1)}) %reduce-scatter.34.cloned.1.call-update) | async-done | bytes 1048592 | tf_op jit(solution)/shard_map/reduce_scatter | solution.py:205
  1807.6 75.8 %reduce-scatter.24.cloned.1.call-done = bf16[256,2048]{1,0:T(8,128)(2,1)} async-done(((bf16[1024,2048]{1,0:T(8,128)(2,1)}), bf16[256,2048]{1,0:T(8,128)(2,1)}) %reduce-scatter.24.cloned.1.call-update) | async-done | bytes 1048592 | tf_op jit(solution)/shard_map/reduce_scatter | solution.py:205
  (1393 shorter events, 772.3 us)
Async XLA Ops:
  7.2 641.1 %copy-start = (bf16[8,2,16,1408]{3,2,1,0:T(8,128)(2,1)S(1)}, bf16[8,2,16,1408]{3,2,1,0:T(8,128)(2,1)}, u32[]{:S(2)}) copy-start(bf16[8,2,16,1408]{3,2,1,0:T(8,128)(2,1)} %param.41) | copy-start | bytes 2162692
  7.2 100.2 %all-gather.18.cloned.1.call-start = ((), (), s32[]{:S(2)}) async-start(), calls=%async_computation.18 | async-start | bytes 3932160 | tf_op jit(solution)/shard_map/all_gather | solution.py:202
  7.9 175.7 %all-gather.28.cloned.1.call-start = ((), (), s32[]{:S(2)}) async-start(), calls=%async_computation.30 | async-start | bytes 5242880 | tf_op jit(solution)/shard_map/all_gather | solution.py:202
  11.0 91.2 %copy-start.316 = (bf16[2,2048]{1,0:T(2,128)(2,1)S(1)}, bf16[2,2048]{1,0:T(2,128)(2,1)}, u32[]{:S(2)}) copy-start(bf16[2,2048]{1,0:T(2,128)(2,1)} %param.30) | copy-start | bytes 24580
  11.0 91.9 %all-to-all-start = ((bf16[4,4,64,512]{3,2,0,1:T(8,128)(2,1)}), bf16[4,4,64,512]{3,2,0,1:T(8,128)(2,1)S(1)}, u32[]{:S(2)}, u32[]{:S(2)}) async-start(bf16[4,4,64,512]{3,2,0,1:T(8,128)(2,1)} %copy_bitcast_fusion), calls=%async_computation | async-start | bytes 2097152 | tf_op jit(solution)/shard_map/all_to_all | solution.py:239
  17.5 303.8 %all-gather.14.cloned.1.call-start = ((), (), s32[]{:S(2)}) async-start(), calls=%async_computation.14 | async-start | bytes 9437184 | tf_op jit(solution)/shard_map/all_gather | solution.py:240
  80.9 209.1 %copy-start.324 = (pred[768]{0:T(1024)(128)(4,1)}, pred[768]{0:T(1024)(128)(4,1)S(1)}, u32[]{:S(2)}) copy-start(pred[768]{0:T(1024)(128)(4,1)S(1)} %get-tuple-element.19) | copy-start | bytes 2308
  80.9 209.1 %copy-start.327 = (pred[768]{0:T(1024)(128)(4,1)}, pred[768]{0:T(1024)(128)(4,1)S(1)}, u32[]{:S(2)}) copy-start(pred[768]{0:T(1024)(128)(4,1)S(1)} %get-tuple-element.20) | copy-start | bytes 2308
  80.9 209.1 %copy-start.330 = (pred[768]{0:T(1024)(128)(4,1)}, pred[768]{0:T(1024)(128)(4,1)S(1)}, u32[]{:S(2)}) copy-start(pred[768]{0:T(1024)(128)(4,1)S(1)} %get-tuple-element.21) | copy-start | bytes 2308
  80.9 209.1 %copy-start.333 = (pred[768]{0:T(1024)(128)(4,1)}, pred[768]{0:T(1024)(128)(4,1)S(1)}, u32[]{:S(2)}) copy-start(pred[768]{0:T(1024)(128)(4,1)S(1)} %get-tuple-element.22) | copy-start | bytes 2308
  81.0 209.1 %copy-start.336 = (pred[768]{0:T(1024)(128)(4,1)}, pred[768]{0:T(1024)(128)(4,1)S(1)}, u32[]{:S(2)}) copy-start(pred[768]{0:T(1024)(128)(4,1)S(1)} %get-tuple-element.23) | copy-start | bytes 2308
  81.0 209.1 %copy-start.339 = (pred[768]{0:T(1024)(128)(4,1)}, pred[768]{0:T(1024)(128)(4,1)S(1)}, u32[]{:S(2)}) copy-start(pred[768]{0:T(1024)(128)(4,1)S(1)} %get-tuple-element.25) | copy-start | bytes 2308
  81.0 209.1 %copy-start.384 = (pred[768]{0:T(1024)(128)(4,1)}, pred[768]{0:T(1024)(128)(4,1)S(1)}, u32[]{:S(2)}) copy-start(pred[768]{0:T(1024)(128)(4,1)S(1)} %get-tuple-element.18) | copy-start | bytes 2308
  81.0 209.1 %copy-start.386 = (pred[768]{0:T(1024)(128)(4,1)}, pred[768]{0:T(1024)(128)(4,1)S(1)}, u32[]{:S(2)}) copy-start(pred[768]{0:T(1024)(128)(4,1)S(1)} %get-tuple-element.24) | copy-start | bytes 2308
  81.7 139.5 %copy-start.342 = (pred[1024]{0:T(1024)(128)(4,1)}, pred[1024]{0:T(1024)(128)(4,1)S(1)}, u32[]{:S(2)}) copy-start(pred[1024]{0:T(1024)(128)(4,1)S(1)} %get-tuple-element.11) | copy-start | bytes 3076
  81.7 139.5 %copy-start.346 = (pred[1024]{0:T(1024)(128)(4,1)}, pred[1024]{0:T(1024)(128)(4,1)S(1)}, u32[]{:S(2)}) copy-start(pred[1024]{0:T(1024)(128)(4,1)S(1)} %get-tuple-element.12) | copy-start | bytes 3076
  81.7 139.5 %copy-start.350 = (pred[1024]{0:T(1024)(128)(4,1)}, pred[1024]{0:T(1024)(128)(4,1)S(1)}, u32[]{:S(2)}) copy-start(pred[1024]{0:T(1024)(128)(4,1)S(1)} %get-tuple-element.13) | copy-start | bytes 3076
  81.7 139.5 %copy-start.354 = (pred[1024]{0:T(1024)(128)(4,1)}, pred[1024]{0:T(1024)(128)(4,1)S(1)}, u32[]{:S(2)}) copy-start(pred[1024]{0:T(1024)(128)(4,1)S(1)} %get-tuple-element.14) | copy-start | bytes 3076
  81.7 139.5 %copy-start.358 = (pred[1024]{0:T(1024)(128)(4,1)}, pred[1024]{0:T(1024)(128)(4,1)S(1)}, u32[]{:S(2)}) copy-start(pred[1024]{0:T(1024)(128)(4,1)S(1)} %get-tuple-element.15) | copy-start | bytes 3076
  81.7 139.5 %copy-start.362 = (pred[1024]{0:T(1024)(128)(4,1)}, pred[1024]{0:T(1024)(128)(4,1)S(1)}, u32[]{:S(2)}) copy-start(pred[1024]{0:T(1024)(128)(4,1)S(1)} %get-tuple-element.17) | copy-start | bytes 3076
  102.2 233.4 %copy-start.13 = (pred[1024,1024]{0,1:T(8,128)(4,1)}, pred[1024,1024]{0,1:T(8,128)(4,1)S(1)}, u32[]{:S(2)}) copy-start(pred[1024,1024]{0,1:T(8,128)(4,1)S(1)} %iota_compare_fusion) | copy-start | bytes 3145732
  102.9 83.9 %copy-start.275 = (f32[1,2048]{1,0:T(1,128)}, f32[1,2048]{1,0:T(1,128)S(1)}, u32[]{:S(2)}) copy-start(f32[1,2048]{1,0:T(1,128)S(1)} %get-tuple-element.149) | copy-start | bytes 24580
  107.3 287.2 %reduce-scatter.26.cloned.1.call-start = ((), (), s32[]{:S(2)}) async-start(), calls=%async_computation.19 | async-start | bytes 3932160 | tf_op jit(solution)/shard_map/reduce_scatter | solution.py:205
  132.9 129.4 %copy-start.321 = (f32[2,8,96]{2,1,0:T(8,128)}, f32[2,8,96]{2,1,0:T(8,128)S(1)}, u32[]{:S(2)}) copy-start(f32[2,8,96]{2,1,0:T(8,128)S(1)} %mul.1071) | copy-start | bytes 18436
  285.6 75.8 %copy-start.240 = (f32[2,1024]{1,0:T(2,128)}, f32[2,1024]{1,0:T(2,128)S(1)}, u32[]{:S(2)}) copy-start(f32[2,1024]{1,0:T(2,128)S(1)} %divide_bitcast_fusion) | copy-start | bytes 24580
  335.5 137.9 %reduce-scatter.22.cloned.1.call-start = ((), (), s32[]{:S(2)}) async-start(), calls=%async_computation.15 | async-start | bytes 5242880 | tf_op jit(solution)/shard_map/reduce_scatter | solution.py:205
  378.0 161.5 %all-gather.20.cloned.1.call-start = ((), (), s32[]{:S(2)}) async-start(), calls=%async_computation.20 | async-start | bytes 3932160 | tf_op jit(solution)/shard_map/all_gather | solution.py:202
  395.9 77.5 %copy-start.15 = (bf16[1,256,2048]{2,1,0:T(8,128)(2,1)S(1)}, bf16[1,256,2048]{2,1,0:T(8,128)(2,1)}, u32[]{:S(2)}) copy-start(bf16[1,256,2048]{2,1,0:T(8,128)(2,1)} %param.21) | copy-start | bytes 3145732
  399.4 140.1 %copy-start.181 = (bf16[2048,4]{0,1:T(4,128)(2,1)S(1)}, bf16[2048,4]{0,1:T(4,128)(2,1)}, u32[]{:S(2)}) copy-start(bf16[2048,4]{0,1:T(4,128)(2,1)} %param.32) | copy-start | bytes 49156
  399.4 209.5 %all-gather.24.cloned.1.call-start = ((), (), s32[]{:S(2)}) async-start(), calls=%async_computation.24 | async-start | bytes 3932160 | tf_op jit(solution)/shard_map/all_gather | solution.py:202
  400.2 373.2 %reduce-scatter.42.cloned.1.call-start = ((), (), s32[]{:S(2)}) async-start(), calls=%async_computation.33 | async-start | bytes 491520
  542.6 226.3 %copy-start.302 = (pred[4,4,192]{2,1,0:T(4,128)(4,1)}, pred[4,4,192]{2,1,0:T(4,128)(4,1)S(1)}, u32[]{:S(2)}) copy-start(pred[4,4,192]{2,1,0:T(4,128)(4,1)S(1)} %copy.508) | copy-start | bytes 9220
  542.9 142.8 %copy-start.290 = (f32[4,4,192]{2,1,0:T(4,128)}, f32[4,4,192]{2,1,0:T(4,128)S(1)}, u32[]{:S(2)}) copy-start(f32[4,4,192]{2,1,0:T(4,128)S(1)} %fusion.425) | copy-start | bytes 36868
  549.3 99.0 %copy-start.253 = (f32[416,16]{0,1:T(8,128)}, f32[416,16]{0,1:T(8,128)S(1)}, u32[]{:S(2)}) copy-start(f32[416,16]{0,1:T(8,128)S(1)} %fusion.647) | copy-start | bytes 79876
  550.5 107.2 %copy-start.249 = (f32[416,16]{0,1:T(8,128)}, f32[416,16]{0,1:T(8,128)S(1)}, u32[]{:S(2)}) copy-start(f32[416,16]{0,1:T(8,128)S(1)} %fusion.650) | copy-start | bytes 79876
  551.1 109.6 %copy-start.255 = (f32[416,16]{0,1:T(8,128)}, f32[416,16]{0,1:T(8,128)S(1)}, u32[]{:S(2)}) copy-start(f32[416,16]{0,1:T(8,128)S(1)} %fusion.642) | copy-start | bytes 79876
  551.7 115.4 %copy-start.245 = (f32[416,16]{0,1:T(8,128)}, f32[416,16]{0,1:T(8,128)S(1)}, u32[]{:S(2)}) copy-start(f32[416,16]{0,1:T(8,128)S(1)} %fusion.648) | copy-start | bytes 79876
  552.3 117.8 %copy-start.251 = (f32[416,16]{0,1:T(8,128)}, f32[416,16]{0,1:T(8,128)S(1)}, u32[]{:S(2)}) copy-start(f32[416,16]{0,1:T(8,128)S(1)} %fusion.640) | copy-start | bytes 79876
  566.7 109.8 %copy-start.243 = (f32[416,16]{0,1:T(8,128)}, f32[416,16]{0,1:T(8,128)S(1)}, u32[]{:S(2)}) copy-start(f32[416,16]{0,1:T(8,128)S(1)} %fusion.649) | copy-start | bytes 79876
  567.3 112.3 %copy-start.247 = (f32[416,16]{0,1:T(8,128)}, f32[416,16]{0,1:T(8,128)S(1)}, u32[]{:S(2)}) copy-start(f32[416,16]{0,1:T(8,128)S(1)} %fusion.641) | copy-start | bytes 79876
  689.1 100.0 %all-gather.16.cloned.1.call-start = ((), (), s32[]{:S(2)}) async-start(), calls=%async_computation.16 | async-start | bytes 5242880 | tf_op jit(solution)/shard_map/all_gather | solution.py:202
  690.8 187.4 %all-gather.30.cloned.1.call-start = ((), (), s32[]{:S(2)}) async-start(), calls=%async_computation.31 | async-start | bytes 5242880 | tf_op jit(solution)/shard_map/all_gather | solution.py:202
  691.4 395.0 %reduce-scatter.32.cloned.1.call-start = ((), (), s32[]{:S(2)}) async-start(), calls=%async_computation.25 | async-start | bytes 3932160 | tf_op jit(solution)/shard_map/reduce_scatter | solution.py:205
  773.3 358.1 %reduce-scatter.40.cloned.1.call-start = ((), (), s32[]{:S(2)}) async-start(), calls=%async_computation.32 | async-start | bytes 655360
  792.7 131.5 %copy-start.379 = (pred[1024,4]{0,1:T(4,128)(4,1)}, pred[1024,4]{0,1:T(4,128)(4,1)S(1)}, u32[]{:S(2)}) copy-start(pred[1024,4]{0,1:T(4,128)(4,1)S(1)} %broadcast_compare_fusion) | copy-start | bytes 12292
  806.1 138.0 %copy-start.197 = (f32[544,16]{0,1:T(8,128)}, f32[544,16]{0,1:T(8,128)S(1)}, u32[]{:S(2)}) copy-start(f32[544,16]{0,1:T(8,128)S(1)} %fusion.651) | copy-start | bytes 104452
  813.9 112.3 %copy-start.185 = (f32[544,16]{0,1:T(8,128)}, f32[544,16]{0,1:T(8,128)S(1)}, u32[]{:S(2)}) copy-start(f32[544,16]{0,1:T(8,128)S(1)} %fusion.653) | copy-start | bytes 104452
  814.6 115.1 %copy-start.189 = (f32[544,16]{0,1:T(8,128)}, f32[544,16]{0,1:T(8,128)S(1)}, u32[]{:S(2)}) copy-start(f32[544,16]{0,1:T(8,128)S(1)} %fusion.645) | copy-start | bytes 104452
  926.2 82.1 %copy-start.293 = (f32[544]{0:T(1024)}, f32[544]{0:T(1024)S(1)}, u32[]{:S(2)}) copy-start(f32[544]{0:T(1024)S(1)} %mul.1046) | copy-start | bytes 6532
  1077.4 85.1 %all-gather.26.cloned.1.call-start = ((), (), s32[]{:S(2)}) async-start(), calls=%async_computation.26 | async-start | bytes 3932160 | tf_op jit(solution)/shard_map/all_gather | solution.py:202
  1091.6 148.6 %reduce-scatter.30.cloned.1.call-start = ((), (), s32[]{:S(2)}) async-start(), calls=%async_computation.22 | async-start | bytes 5242880 | tf_op jit(solution)/shard_map/reduce_scatter | solution.py:205
  1126.2 202.1 %all-gather.22.cloned.1.call-start = ((), (), s32[]{:S(2)}) async-start(), calls=%async_computation.23 | async-start | bytes 5242880 | tf_op jit(solution)/shard_map/all_gather | solution.py:202
  1246.8 364.2 %reduce-scatter.38.cloned.1.call-start = ((), (), s32[]{:S(2)}) async-start(), calls=%async_computation.29 | async-start | bytes 573440 | tf_op jit(solution)/shard_map/reduce_scatter | solution.py:384
  1467.5 203.2 %reduce-scatter.46.cloned.1.call-start = ((), (), s32[]{:S(2)}) async-start(), calls=%async_computation.35 | async-start | bytes 491520
  1486.6 185.8 %reduce-scatter.36.cloned.1.call-start = ((), (), s32[]{:S(2)}) async-start(), calls=%async_computation.28 | async-start | bytes 3932160 | tf_op jit(solution)/shard_map/reduce_scatter | solution.py:205
  1511.4 164.3 %reduce-scatter.28.cloned.1.call-start = ((), (), s32[]{:S(2)}) async-start(), calls=%async_computation.21 | async-start | bytes 3932160 | tf_op jit(solution)/shard_map/reduce_scatter | solution.py:205
  1546.2 134.4 %reduce-scatter.44.cloned.1.call-start = ((), (), s32[]{:S(2)}) async-start(), calls=%async_computation.34 | async-start | bytes 655360
  1595.2 129.8 %all-reduce.3.cloned.1.call-start = ((), (), s32[]{:S(2)}) async-start(), calls=%async_computation.36 | async-start | bytes 5046272 | tf_op jit(solution)/shard_map/psum | solution.py:391
  1614.9 188.8 %reduce-scatter.34.cloned.1.call-start = ((), (), s32[]{:S(2)}) async-start(), calls=%async_computation.27 | async-start | bytes 5242880 | tf_op jit(solution)/shard_map/reduce_scatter | solution.py:205
  1632.9 250.5 %reduce-scatter.24.cloned.1.call-start = ((), (), s32[]{:S(2)}) async-start(), calls=%async_computation.17 | async-start | bytes 5242880 | tf_op jit(solution)/shard_map/reduce_scatter | solution.py:205
  1732.0 151.4 %copy-start.41 = (bf16[256,2048]{1,0:T(8,128)(2,1)S(1)}, bf16[256,2048]{1,0:T(8,128)(2,1)}, u32[]{:S(2)}) copy-start(bf16[256,2048]{1,0:T(8,128)(2,1)} %reduce-scatter.22.cloned.1.call-done) | copy-start | bytes 3145732
  1732.0 151.4 %copy-start.375 = (f32[256]{0:T(256)S(1)}, f32[256]{0:T(256)}, u32[]{:S(2)}) copy-start(f32[256]{0:T(256)} %get-tuple-element.155) | copy-start | bytes 3076
  1732.0 151.4 %copy-start.393 = (f32[256]{0:T(256)S(1)}, f32[256]{0:T(256)}, u32[]{:S(2)}) copy-start(f32[256]{0:T(256)} %get-tuple-element.154) | copy-start | bytes 3076
  1732.0 151.4 %copy-start.399 = (f32[256]{0:T(256)S(1)}, f32[256]{0:T(256)}, u32[]{:S(2)}) copy-start(f32[256]{0:T(256)} %copy-done.398) | copy-start | bytes 3076
  (395 other events, 2813.9 us)
Sparse Core Ops, SparseCore 0:
  9.6 92.4 all-gather.17
  103.7 79.8 all-gather.27
  186.1 52.9 all-gather.13
  335.6 58.7 reduce-scatter.25
  396.6 76.7 reduce-scatter.21
  475.5 63.9 all-gather.19
  541.2 62.1 all-gather.23
  689.2 19.2 reduce-scatter.41
  710.1 78.9 all-gather.15
  790.6 79.2 all-gather.29
  872.2 58.7 reduce-scatter.31
  1077.5 21.0 reduce-scatter.39
  1100.7 61.7 all-gather.25
  1164.6 75.4 reduce-scatter.29
  1246.9 81.2 all-gather.21
  1467.6 19.5 reduce-scatter.37
  1489.3 18.9 reduce-scatter.45
  1511.5 58.7 reduce-scatter.35
  1572.8 60.2 reduce-scatter.27
  1635.3 21.6 reduce-scatter.43
  1661.8 63.1 all-reduce.2
  1727.3 76.3 reduce-scatter.33
  1806.1 77.2 reduce-scatter.23
